TPU v7x, 128 devices: a whole 4x4x4 slice. The times are simulated.
128 devices in a mesh: grp: 4 (over x), seq: 32 (over z, y, core).
Axes of the slice: x: 4, y: 4, z: 4, core: 2. Of those that a mesh axis runs over, the one named last changes fastest.
Arguments:
- video_q: bfloat16 [65536, 1536], P(('grp', 'seq')), may hold values from -30 to 30
- video_k: bfloat16 [65536, 1536], P(('grp', 'seq')), may hold values from -30 to 30
- video_v: bfloat16 [65536, 1536], P(('grp', 'seq')), may hold values from -6 to 6
- audio_q: bfloat16 [8192, 1536], P(('grp', 'seq')), may hold values from -30 to 30
- audio_k: bfloat16 [8192, 1536], P(('grp', 'seq')), may hold values from -30 to 30
- audio_v: bfloat16 [8192, 1536], P(('grp', 'seq')), may hold values from -6 to 6
- video_clip: int32 [65536], P(('grp', 'seq')), may hold values from 0 to 35, as said below
- audio_clip: int32 [8192], P(('grp', 'seq')), may hold values from 0 to 35, as said below
Outputs:
- video_out: bfloat16 [65536, 1536], P(('grp', 'seq'))
- audio_out: bfloat16 [8192, 1536], P(('grp', 'seq'))
Inputs may be any that keep to these rules, and one draw needn't show every extreme that they name: `video_clip`: group g (0 to 3) holds clips g * 9 to g * 9 + 8. Its audio tokens are the block of 2048 rows from ((g + 1) mod 4) * 64 * 32 on, in clip order; in every group one clip has exactly (17) * 64 audio tokens and each other clip has 64 to 128. Its video tokens are rows g * 512 * 32 onward, in clip order, each clip with exactly 8 times as many video tokens as audio tokens. `audio_clip`: see video_clip.
All inputs are finite; a program needn't handle non-finite values.
Results may differ from a plain program's by a relative error of at most 0.018.
Values may be sent and summed in bfloat16 or wider, within the bound.
A program may use at most 256 MiB of HBM per device.

v0:
```python
import math

import jax
import jax.numpy as jnp
from jax import lax
from jax.sharding import PartitionSpec as P

HD = 128


def shifted(array, axis, by):
    length = lax.axis_size(axis)
    return lax.ppermute(array, axis, [(i, (i + by) % length) for i in range(length)])


def partial_rows(queries, clips, video_k, video_v, video_clip, head_count, score_scale):
    query_rows = queries.shape[0]
    video_rows = video_k.shape[0]
    scores = (
        jnp.einsum(
            "qhd,khd->hqk",
            queries.reshape(query_rows, head_count, HD),
            video_k.reshape(video_rows, head_count, HD),
            preferred_element_type=jnp.float32,
        )
        * score_scale
    )
    allowed = clips[:, None] == video_clip[None, :]
    scores = jnp.where(allowed[None], scores, -jnp.inf)
    local_high = jnp.maximum(jnp.max(scores, axis=2), -1e30)
    weights = jnp.exp(scores - local_high[:, :, None])
    local_total = jnp.sum(weights, axis=2).T
    local_out = jnp.einsum(
        "hqk,khd->qhd",
        weights.astype(jnp.bfloat16),
        video_v.reshape(video_rows, head_count, HD),
        preferred_element_type=jnp.float32,
    )
    return (local_out, local_high.T, local_total)


def on_device(video_q, video_k, video_v, audio_q, audio_k, audio_v, video_clip, audio_clip):
    head_count = video_q.shape[1] // HD
    score_scale = 1.0 / math.sqrt(HD)
    moved_q, moved_k, moved_v, moved_clip = shifted(
        (audio_q, audio_k, audio_v, audio_clip), "grp", -1
    )
    video_rows = video_q.shape[0]
    video_split = video_q.reshape(video_rows, head_count, HD)
    highest = jnp.full((head_count, video_rows), -1e30, jnp.float32)
    accumulated = jnp.zeros((video_rows, head_count, HD), jnp.float32)
    key_part = lax.all_gather(moved_k, "seq", axis=0, tiled=True)
    value_part = lax.all_gather(moved_v, "seq", axis=0, tiled=True)
    clip_part = lax.all_gather(moved_clip, "seq", axis=0, tiled=True)
    key_rows = key_part.shape[0]
    scores = (
        jnp.einsum(
            "qhd,khd->hqk",
            video_split,
            key_part.reshape(key_rows, head_count, HD),
            preferred_element_type=jnp.float32,
        )
        * score_scale
    )
    allowed = video_clip[:, None] == clip_part[None, :]
    scores = jnp.where(allowed[None], scores, -jnp.inf)
    newest = jnp.maximum(highest, jnp.max(scores, axis=2))
    weights = jnp.exp(scores - newest[:, :, None])
    shrink = jnp.exp(highest - newest)
    running = jnp.sum(weights, axis=2)
    contrib = jnp.einsum(
        "hqk,khd->qhd",
        weights.astype(jnp.bfloat16),
        value_part.reshape(key_rows, head_count, HD),
        preferred_element_type=jnp.float32,
    )
    accumulated = accumulated * shrink.T[:, :, None] + contrib
    highest, running, accumulated = (newest, running, accumulated)
    video_out = (
        (accumulated / running.T[:, :, None])
        .reshape(video_rows, head_count * HD)
        .astype(jnp.bfloat16)
    )
    all_queries, all_clips = (
        lax.all_gather(moved_q, "seq", axis=0, tiled=True),
        lax.all_gather(moved_clip, "seq", axis=0, tiled=True),
    )
    all_rows = all_queries.shape[0]
    own_rows = moved_q.shape[0]
    local_out, local_high, local_total = partial_rows(
        all_queries, all_clips, video_k, video_v, video_clip, head_count, score_scale
    )
    outputs, highs, totals = (
        lax.all_to_all(
            local_out.reshape(all_rows, 1, head_count * HD),
            "seq",
            split_axis=0,
            concat_axis=1,
            tiled=True,
        ),
        lax.all_to_all(local_high[:, None, :], "seq", split_axis=0, concat_axis=1, tiled=True),
        lax.all_to_all(local_total[:, None, :], "seq", split_axis=0, concat_axis=1, tiled=True),
    )
    overall = jnp.max(highs, axis=1)
    factor = jnp.exp(highs - overall[:, None, :])
    summed_total = jnp.sum(totals * factor, axis=1)
    pieces = outputs.reshape(own_rows, outputs.shape[1], head_count, HD)
    summed = jnp.sum(pieces * factor[:, :, :, None], axis=1)
    audio_here = (
        (summed / summed_total[:, :, None]).reshape(own_rows, head_count * HD).astype(jnp.bfloat16)
    )
    audio_out = shifted(audio_here, "grp", 1)
    return (video_out, audio_out)


def solution(mesh):
    return jax.shard_map(
        on_device,
        mesh=mesh,
        in_specs=(
            P(("grp", "seq"), None),
            P(("grp", "seq"), None),
            P(("grp", "seq"), None),
            P(("grp", "seq"), None),
            P(("grp", "seq"), None),
            P(("grp", "seq"), None),
            P(("grp", "seq")),
            P(("grp", "seq")),
        ),
        out_specs=(P(("grp", "seq"), None), P(("grp", "seq"), None)),
        check_vma=False,
    )
```

profile of v0, /device:TPU:0, one launch (start us, length us, event | category | flops | bytes accessed | tf_op | source)
XLA Modules:
  0.0 423.1 jit_solution(2121954428421242907)
XLA Ops:
  7.2 0.0 all-gather.8.cloned.1.call-start
  7.2 2.9 collective-permute-start.3
  10.1 4.5 %collective-permute-done.3 = bf16[64,1536]{1,0:T(8,128)(2,1)S(1)} collective-permute-done((bf16[64,1536]{1,0:T(8,128)(2,1)}, bf16[64,1536]{1,0:T(8,128)(2,1)S(1)}, u32[]{:S(2)}, u32[]{:S(2)}) %collective-permute-start.3) | collective-permute-done | bytes 196640 | tf_op jit(solution)/shard_map/ppermute | solution.py:13
  14.6 0.7 copy-done.2
  15.3 0.0 all-gather.8.cloned.1.call-update
  15.3 0.0 all-gather.4.cloned.1.call-start
  15.3 3.7 collective-permute-start.1
  19.0 3.6 collective-permute-done.1
  22.6 0.7 copy-done
  23.3 0.0 all-gather.4.cloned.1.call-update
  23.3 0.0 all-gather.6.cloned.1.call-start
  23.4 3.7 collective-permute-start
  27.0 0.1 collective-permute-start.2
  27.1 1.7 copy.94
  28.8 1.2 dynamic-slice
  30.8 0.3 dynamic-update-slice
  31.0 18.4 %all-reduce = s32[2048]{0:T(1024)S(1)} all-reduce(s32[2048]{0:T(1024)S(1)} %dynamic-update-slice), channel_id=1, replica_groups=mesh['grp'=4,'seq'=32] {'seq'}, use_global_device_ids=true, to_apply=%add | all-reduce | flops 2048 | bytes 16384
  49.5 1.3 broadcast_compare_fusion
  50.8 0.7 copy-done.1
  51.5 16.3 %all-gather.8.cloned.1.call-done = bf16[2048,1536]{1,0:T(8,128)(2,1)} async-done(((bf16[64,1536]{1,0:T(8,128)(2,1)}), bf16[2048,1536]{1,0:T(8,128)(2,1)}) %all-gather.8.cloned.1.call-update) | async-done | bytes 6291472 | tf_op jit(solution)/shard_map/all_gather | solution.py:85
  67.8 8.7 %copy.93 = bf16[2048,1536]{0,1:T(8,128)(2,1)} copy(bf16[2048,1536]{1,0:T(8,128)(2,1)} %all-gather.8.cloned.1.call-done) | data formatting | bytes 12582912 | tf_op jit(solution)/shard_map/all_gather | solution.py:85
  76.5 21.3 %fusion.1 = (f32[12,2048]{1,0:T(8,128)S(1)}, f32[12,2048,512]{1,2,0:T(8,128)}) fusion(pred[2048,512]{0,1:T(8,128)(4,1)S(1)} %broadcast_compare_fusion, bf16[2048,12,128]{0,2,1:T(8,128)(2,1)} %bitcast.59, bf16[512,12,128]{0,2,1:T(8,128)(2,1)S(1)} %bitcast.63), kind=kOutput, calls=%fused_computation.5 | convolution fusion | flops 3258949632 | bytes 59342848 | tf_op jit(solution)/shard_map/qhd,khd->hqk/dot_general | solution.py:20
  97.8 22.1 %fusion.4 = f32[12,2048]{1,0:T(8,128)S(1)} fusion(f32[12,2048,512]{1,2,0:T(8,128)} %get-tuple-element.23, f32[12,2048]{1,0:T(8,128)S(1)} %get-tuple-element.17, pred[2048,512]{0,1:T(8,128)(4,1)S(1)} %broadcast_compare_fusion), kind=kLoop, calls=%fused_computation.8 | loop fusion | flops 50307072 | bytes 51576832 | tf_op jit(solution)/shard_map/reduce_sum | solution.py:32
  119.8 0.5 broadcast.69
  120.4 0.6 reduce.2
  121.0 0.4 copy.123
  121.4 1.6 reshape.121
  122.9 4.8 %all-to-all-start.2 = ((f32[32,1,768]{2,1,0:T(1,128)}), f32[32,1,768]{2,1,0:T(1,128)S(1)}, u32[]{:S(2)}, u32[]{:S(2)}) async-start(f32[32,1,768]{2,1,0:T(1,128)} %reshape.121), calls=%async_computation.2 | async-start | bytes 196608 | tf_op jit(solution)/shard_map/all_to_all | solution.py:102
  127.7 2.6 copy.97
  130.3 0.6 reduce.4
  130.9 0.4 copy.124
  131.3 1.6 reshape.119
  132.9 2.4 all-to-all-done.2
  135.3 5.2 %all-to-all-start.1 = ((f32[32,1,768]{2,1,0:T(1,128)}), f32[32,1,768]{2,1,0:T(1,128)S(1)}, u32[]{:S(2)}, u32[]{:S(2)}) async-start(f32[32,1,768]{2,1,0:T(1,128)} %reshape.119), calls=%async_computation.1 | async-start | bytes 196608 | tf_op jit(solution)/shard_map/all_to_all | solution.py:101
  140.5 24.7 %fusion.6 = f32[12,2048,128]{1,2,0:T(8,128)} fusion(bf16[512,12,128]{0,2,1:T(8,128)(2,1)} %bitcast.67, f32[12,2048,512]{1,2,0:T(8,128)} %get-tuple-element.23, f32[12,2048]{1,0:T(8,128)S(1)} %get-tuple-element.17, pred[2048,512]{0,1:T(8,128)(4,1)S(1)} %broadcast_compare_fusion), kind=kOutput, calls=%fused_computation.10 | convolution fusion | flops 3271557120 | bytes 65634304 | tf_op jit(solution)/shard_map/hqk,khd->qhd/dot_general | solution.py:33
  165.2 30.7 %copy.99 = f32[2048,1,1536]{2,1,0:T(1,128)} copy(f32[2048,1,1536]{0,2,1:T(8,128)} %bitcast.60) | data formatting | bytes 25165824 | tf_op jit(solution)/shard_map/reshape | solution.py:95
  195.8 7.6 %all-to-all-start = ((f32[2048,1,1536]{2,1,0:T(1,128)}), f32[2048,1,1536]{2,1,0:T(1,128)}, u32[]{:S(2)}, u32[]{:S(2)}) async-start(f32[2048,1,1536]{2,1,0:T(1,128)} %copy.99), calls=%async_computation | async-start | bytes 25165824 | tf_op jit(solution)/shard_map/all_to_all | solution.py:94
  203.5 1.7 copy.88
  205.2 0.7 broadcast_compare_fusion.1
  205.9 0.0 all-gather.4.cloned.1.call-done
  205.9 8.7 %copy.89 = bf16[2048,1536]{0,1:T(8,128)(2,1)} copy(bf16[2048,1536]{1,0:T(8,128)(2,1)} %all-gather.4.cloned.1.call-done) | data formatting | bytes 12582912 | tf_op jit(solution)/shard_map/all_gather | solution.py:52
  214.6 8.7 %copy.92 = bf16[2048,1536]{0,1:T(8,128)(2,1)} copy(bf16[2048,1536]{1,0:T(8,128)(2,1)} %all-gather.6.cloned.1.call-done) | data formatting | bytes 12582912 | tf_op jit(solution)/shard_map/all_gather | solution.py:53
  223.3 21.0 %fusion = (f32[12,512]{1,0:T(8,128)S(1)}, f32[12,512,2048]{2,1,0:T(8,128)}) fusion(pred[512,2048]{1,0:T(8,128)(4,1)S(1)} %broadcast_compare_fusion.1, bf16[512,12,128]{0,2,1:T(8,128)(2,1)S(1)} %bitcast.61, bf16[2048,12,128]{0,2,1:T(8,128)(2,1)} %bitcast.58), kind=kOutput, calls=%fused_computation.4 | convolution fusion | flops 3258968064 | bytes 59269120 | tf_op jit(solution)/shard_map/qhd,khd->hqk/dot_general | solution.py:57
  244.4 21.9 %fusion.2 = f32[12,512]{1,0:T(8,128)S(1)} fusion(f32[12,512,2048]{2,1,0:T(8,128)} %get-tuple-element.21, f32[12,512]{1,0:T(8,128)S(1)} %get-tuple-element.19, pred[512,2048]{1,0:T(8,128)(4,1)S(1)} %broadcast_compare_fusion.1), kind=kLoop, calls=%fused_computation.6 | loop fusion | flops 50325504 | bytes 51429376 | tf_op jit(solution)/shard_map/reduce_sum | solution.py:70
  266.3 0.8 reduce.5
  267.1 1.7 reshape.120
  268.9 0.4 copy.114
  269.3 0.8 reduce.3
  270.1 1.7 reshape.122
  271.8 0.4 copy.106
  272.3 0.1 fusion.18
  272.4 0.1 copy.107
  272.4 1.0 copy.102
  273.4 8.4 %mul.36 = f32[64,32,12,128]{3,2,1,0:T(8,128)} broadcast(f32[64,32,12]{2,1,0:T(8,128)S(1)} %copy.102), dimensions={0,1,2} | broadcast | bytes 12681216 | tf_op jit(solution)/shard_map/mul | solution.py:108
  281.8 15.6 %mul.37 = f32[64,32,1,1536]{3,1,0,2:T(8,128)} reshape(f32[64,32,12,128]{3,2,1,0:T(8,128)} %mul.36) | data formatting | bytes 25165824 | tf_op jit(solution)/shard_map/mul | solution.py:108
  297.4 66.9 %all-to-all-done = f32[2048,1,1536]{2,1,0:T(1,128)} async-done(((f32[2048,1,1536]{2,1,0:T(1,128)}), f32[2048,1,1536]{2,1,0:T(1,128)}, u32[]{:S(2)}, u32[]{:S(2)}) %all-to-all-start) | async-done | bytes 12582944 | tf_op jit(solution)/shard_map/all_to_all | solution.py:94
  364.3 10.3 %copy.117 = f32[2048,1,1536]{2,0,1:T(8,128)} copy(f32[2048,1,1536]{2,1,0:T(1,128)} %all-to-all-done) | data formatting | bytes 25165824
  374.6 14.6 %fusion.12 = f32[64,1536]{1,0:T(8,128)S(1)} fusion(f32[64,32,1,1536]{3,0,1,2:T(8,128)} %bitcast.57, f32[64,32,1,1536]{3,1,0,2:T(8,128)} %mul.37), kind=kLoop, calls=%fused_computation.15 | loop fusion | flops 6193152 | bytes 25559040 | tf_op jit(solution)/shard_map/reduce_sum | solution.py:108
  389.3 0.2 div.21
  389.5 0.2 fusion.17
  389.6 1.5 collective-permute-start.4
  391.2 23.1 %fusion.14 = bf16[512,12,128]{0,2,1:T(8,128)(2,1)S(1)} fusion(bf16[2048,12,128]{0,2,1:T(8,128)(2,1)} %bitcast.62, f32[12,512,2048]{2,1,0:T(8,128)} %get-tuple-element.21, f32[12,512]{1,0:T(8,128)S(1)} %get-tuple-element.19, pred[512,2048]{1,0:T(8,128)(4,1)S(1)} %broadcast_compare_fusion.1, f32[512,12]{0,1:T(8,128)S(1)} %bitcast.70, ...), kind=kOutput, calls=%fused_computation.18 | convolution fusion | flops 3273916416 | bytes 59318272 | tf_op jit(solution)/shard_map/hqk,khd->qhd/dot_general | solution.py:71
  414.3 1.6 copy.108
  415.9 0.7 copy.127
  (15 shorter events, 0.1 us)
Async XLA Ops:
  7.2 60.6 %all-gather.8.cloned.1.call-start = ((), (), s32[]{:S(2)}) async-start(), calls=%async_computation.5 | async-start | bytes 6488064 | tf_op jit(solution)/shard_map/all_gather | solution.py:85
  7.2 7.4 %collective-permute-start.3 = (bf16[64,1536]{1,0:T(8,128)(2,1)}, bf16[64,1536]{1,0:T(8,128)(2,1)S(1)}, u32[]{:S(2)}, u32[]{:S(2)}) collective-permute-start(bf16[64,1536]{1,0:T(8,128)(2,1)} %param.11), channel_id=1, source_target_pairs={{0,96},{32,0},{64,32},{96,64},{1,97},{33,1},{65,33},{97,65},{2,98}... | collective-permute-start | bytes 589832 | tf_op jit(solution)/shard_map/ppermute | solution.py:13
  14.6 0.7 copy-start.2
  15.3 190.6 %all-gather.4.cloned.1.call-start = ((), (), s32[]{:S(2)}) async-start(), calls=%async_computation.3 | async-start | bytes 6488064 | tf_op jit(solution)/shard_map/all_gather | solution.py:52
  15.3 7.3 %collective-permute-start.1 = (bf16[64,1536]{1,0:T(8,128)(2,1)}, bf16[64,1536]{1,0:T(8,128)(2,1)S(1)}, u32[]{:S(2)}, u32[]{:S(2)}) collective-permute-start(bf16[64,1536]{1,0:T(8,128)(2,1)} %param.12), channel_id=1, source_target_pairs={{0,96},{32,0},{64,32},{96,64},{1,97},{33,1},{65,33},{97,65},{2,98}... | collective-permute-start | bytes 589832 | tf_op jit(solution)/shard_map/ppermute | solution.py:13
  22.6 0.7 copy-start
  23.3 191.3 %all-gather.6.cloned.1.call-start = ((), (), s32[]{:S(2)}) async-start(), calls=%async_computation.4 | async-start | bytes 6488064 | tf_op jit(solution)/shard_map/all_gather | solution.py:53
  23.4 7.4 %collective-permute-start = (s32[64]{0:T(128)}, s32[64]{0:T(128)S(1)}, u32[]{:S(2)}, u32[]{:S(2)}) collective-permute-start(s32[64]{0:T(128)} %param.15), channel_id=1, source_target_pairs={{0,96},{32,0},{64,32},{96,64},{1,97},{33,1},{65,33},{97,65},{2,98}... | collective-permute-start | bytes 776 | tf_op jit(solution)/shard_map/ppermute | solution.py:13
  27.0 23.8 %collective-permute-start.2 = (bf16[64,1536]{1,0:T(8,128)(2,1)}, bf16[64,1536]{1,0:T(8,128)(2,1)S(1)}, u32[]{:S(2)}, u32[]{:S(2)}) collective-permute-start(bf16[64,1536]{1,0:T(8,128)(2,1)} %param.13), channel_id=1, source_target_pairs={{0,96},{32,0},{64,32},{96,64},{1,97},{33,1},{65,33},{97,65},{2,98}... | collective-permute-start | bytes 589832 | tf_op jit(solution)/shard_map/ppermute | solution.py:13
  50.8 0.7 copy-start.1
  122.9 12.3 %all-to-all-start.2 = ((f32[32,1,768]{2,1,0:T(1,128)}), f32[32,1,768]{2,1,0:T(1,128)S(1)}, u32[]{:S(2)}, u32[]{:S(2)}) async-start(f32[32,1,768]{2,1,0:T(1,128)} %reshape.121), calls=%async_computation.2 | async-start | bytes 196608 | tf_op jit(solution)/shard_map/all_to_all | solution.py:102
  135.3 60.6 %all-to-all-start.1 = ((f32[32,1,768]{2,1,0:T(1,128)}), f32[32,1,768]{2,1,0:T(1,128)S(1)}, u32[]{:S(2)}, u32[]{:S(2)}) async-start(f32[32,1,768]{2,1,0:T(1,128)} %reshape.119), calls=%async_computation.1 | async-start | bytes 196608 | tf_op jit(solution)/shard_map/all_to_all | solution.py:101
  195.8 9.4 %copy-start.3 = (s32[512]{0:T(512)S(1)}, s32[512]{0:T(512)}, u32[]{:S(2)}) copy-start(s32[512]{0:T(512)} %param.14) | copy-start | bytes 6148
  195.8 168.5 %all-to-all-start = ((f32[2048,1,1536]{2,1,0:T(1,128)}), f32[2048,1,1536]{2,1,0:T(1,128)}, u32[]{:S(2)}, u32[]{:S(2)}) async-start(f32[2048,1,1536]{2,1,0:T(1,128)} %copy.99), calls=%async_computation | async-start | bytes 25165824 | tf_op jit(solution)/shard_map/all_to_all | solution.py:94
  389.6 26.2 %collective-permute-start.4 = (bf16[64,1536]{1,0:T(8,128)(2,1)S(1)}, bf16[64,1536]{1,0:T(8,128)(2,1)S(1)}, u32[]{:S(2)}, u32[]{:S(2)}) collective-permute-start(bf16[64,1536]{1,0:T(8,128)(2,1)S(1)} %fusion.17), channel_id=1, source_target_pairs={{0,32},{32,64},{64,96},{96,0},{1,33},{33,65},{65,97},{97,1},{2,34}... | collective-permute-start | bytes 589832 | tf_op jit(solution)/shard_map/ppermute | solution.py:13
Sparse Core Ops, SparseCore 0:
  15.4 52.3 all-gather.7
  70.0 48.1 all-gather.3
  121.0 48.1 all-gather.5
where the time goes:
time: 426 us; the launch traced here: 423 us
  local copies, waits for them, and re-layouts  113 us (27%)
  waiting for transfers between devices  93.7 us (22%)
  matrix products  90.1 us (21%)
  other arithmetic  63.8 us (15%)
  starting transfers between devices  29.5 us (7%)
  blocking collectives  18.4 us (4%)
  between operations  14.7 us (3%)
    all_to_all x1, waiting for transfers between devices, on_device(): lax.all_to_all(local_out.reshape(all_rows, 1, head_count * HD), 'seq', sp...  66.9 us
    reshape x1, local copies, waits for them, and re-layouts, on_device(): local_out.reshape(all_rows, 1, head_count * HD)  30.7 us
    unnamed x23, local copies, waits for them, and re-layouts  29.5 us
    dot_general x1, matrix products, partial_rows(): jnp.einsum('hqk,khd->qhd', weights.astype(jnp.bfloat16), video_v.reshape(...  24.7 us
    mul x2, local copies, waits for them, and re-layouts, on_device(): summed = jnp.sum(pieces * factor[:, :, :, None], axis=1)  24 us
    dot_general x1, matrix products, on_device(): jnp.einsum('hqk,khd->qhd', weights.astype(jnp.bfloat16), value_part.resha...  23.1 us
    reduce_sum x1, other arithmetic, partial_rows(): local_total = jnp.sum(weights, axis=2).T  22.1 us
    reduce_sum x1, other arithmetic, on_device(): running = jnp.sum(weights, axis=2)  21.9 us
  transfers between devices with their start and end apart: 11, of which 5 were waited for; matrix products, arithmetic and copies ran while one was open for 56% of the time, Pallas kernels for 0%

commit v1 on v0

v1 whole, which is shorter than its diff:
```python
import math

import jax
import jax.numpy as jnp
from jax import lax
from jax.experimental import pallas as pl
from jax.experimental.pallas import tpu as pltpu
from jax.sharding import PartitionSpec as P

MESH = pl.DeviceIdType.MESH
BF = jnp.bfloat16
F32 = jnp.float32
HD = 128
CLIPS = 9
SCALE = math.log2(math.e) / math.sqrt(HD)
FAR = -1048576.0
LOW = -32768.0
BLOCKS = 10
STAT = 3 * HD
ROWS = STAT + 16


def kernel(
    first_ref, vq_hbm, vk_hbm, vv_hbm, ve_hbm, aq_hbm, ak_hbm, av_hbm,
    vout_hbm, aout_hbm,
    vq, vk, vv, ve, aq, ak, av, vt, window, part, got1, got2, vo, ao,
    x_send, x_recv, g_send, g_recv, v_send, v_recv, v_local, r_send, r_recv, o_send, o_recv, o_local,
):
    g = lax.axis_index("grp")
    s = lax.axis_index("seq")
    core = lax.rem(s, 2)
    chip = s // 2
    z, y = chip // 4, lax.rem(chip, 4)
    zp, zm, z2 = lax.rem(z + 1, 4), lax.rem(z + 3, 4), lax.rem(z + 2, 4)
    yp, ym, y2 = lax.rem(y + 1, 4), lax.rem(y + 3, 4), lax.rem(y + 2, 4)
    gp, gm = lax.rem(g + 1, 4), lax.rem(g + 3, 4)

    def device(grp, zz, yy, cc):
        return (grp, (zz * 4 + yy) * 2 + cc)

    other = device(g, z, y, 1 - core)
    to_yp, to_ym, to_y2 = (device(g, z, b, core) for b in (yp, ym, y2))
    to_zp, to_zm, to_z2 = (device(g, b, y, core) for b in (zp, zm, z2))
    before = lax.rem(chip + 15, 16)
    after = lax.rem(chip + 1, 16)
    result_low = (gp, chip * 2)
    result_high = (gp, before * 2 + 1)

    barrier = pltpu.get_barrier_semaphore()

    def greet(dev):
        pl.semaphore_signal(barrier, inc=1, device_id=dev, device_id_type=MESH)

    for dev in (other, to_yp, to_ym, to_y2, to_zp, to_zm, to_z2):
        greet(dev)
    for cc in (0, 1):
        greet(device(gm, z, y, cc))
        greet(device(gp, z, y, cc))
    greet(result_high)

    @pl.when(core == 1)
    def _():
        greet((gm, after * 2))
        greet((gm, after * 2 + 1))

    pl.semaphore_wait(barrier, 12 + 2 * core)

    def remote(src, dst, ssem, rsem, dev):
        return pltpu.make_async_remote_copy(
            src_ref=src, dst_ref=dst, send_sem=ssem, recv_sem=rsem, device_id=dev, device_id_type=MESH
        )

    def columns(half, width):
        return pl.ds(pl.multiple_of(half * width, 128), width)

    tensors = ((aq_hbm, aq, 896), (ak_hbm, ak, 768), (av_hbm, av, 768))

    def x_step(t):
        src, dst, width = tensors[t]
        return [
            remote(
                src.at[:, pl.ds(cc * width, width)], dst.at[core, z, y], x_send.at[t, cc],
                x_recv.at[t, core], device(gm, z, y, cc),
            )
            for cc in (0, 1)
        ]

    def x_wait(t):
        src, dst, width = tensors[t]
        for cc in (0, 1):
            remote(
                src.at[:, pl.ds(cc * width, width)], dst.at[cc, z, y], x_send.at[t, cc],
                x_recv.at[t, cc], device(gm, z, y, cc),
            ).wait_recv()

    def gather(t, stage):
        x = tensors[t][1]
        low, high = pl.ds(0, 32), pl.ds(32, 32)
        first, last = pl.ds(0, 2), pl.ds(2, 2)
        plan = (
            (x.at[0, z, y], to_yp),
            (x.at[0, z, y], to_ym),
            (x.at[1, z, y], to_zp),
            (x.at[1, z, y], to_zm),
        ), (
            (x.at[0, z, ym, low], to_yp),
            (x.at[0, z, yp, high], to_ym),
            (x.at[1, zm, y, low], to_zp),
            (x.at[1, zp, y, high], to_zm),
        ), (
            (x.at[0, z], to_zp),
            (x.at[0, z], to_zm),
            (x.at[1, :, y], to_yp),
            (x.at[1, :, y], to_ym),
        ), (
            (x.at[0, zm, first], to_zp),
            (x.at[0, zp, last], to_zm),
            (x.at[1, first, ym], to_yp),
            (x.at[1, last, yp], to_ym),
        )
        return [
            remote(ref, ref, g_send.at[t, stage * 4 + i], g_recv.at[t, stage * 4 + i], dev)
            for i, (ref, dev) in enumerate(plan[stage])
        ]

    def start(copies):
        for copy in copies:
            copy.start()

    def arrive(copies):
        for copy in copies:
            copy.wait_recv()

    def sent(copies):
        for copy in copies:
            copy.wait_send()

    video = ((vk_hbm, vk), (vv_hbm, vv), (vq_hbm, vq))
    own_rows = pl.ds(pl.multiple_of(core * 512, 512), 512)
    other_rows = pl.ds(pl.multiple_of((1 - core) * 512, 512), 512)

    def swap(i):
        if i == 3:
            return (
                remote(ve_hbm, ve.at[own_rows], v_send.at[3], v_recv.at[3], other),
                pltpu.make_async_copy(ve_hbm, ve.at[own_rows], v_local.at[3]),
            )
        src, dst = video[i]
        return (
            remote(src.at[:, columns(1 - core, 768)], dst.at[own_rows], v_send.at[i], v_recv.at[i], other),
            pltpu.make_async_copy(src.at[:, columns(core, 768)], dst.at[own_rows], v_local.at[i]),
        )

    def swap_start(i):
        away, here = swap(i)
        away.start()
        here.start()

    def swap_wait(i):
        away, here = swap(i)
        away.wait_recv()
        here.wait()

    start(x_step(0))
    swap_start(3)
    swap_start(0)
    swap_start(1)
    start(x_step(1))
    start(x_step(2))
    swap_start(2)

    x_wait(0)
    start(gather(0, 0))
    arrive(gather(0, 0))
    start(gather(0, 1))
    arrive(gather(0, 1))
    start(gather(0, 2))
    x_wait(1)
    start(gather(1, 0))

    swap_wait(1)

    def turn(h, carry):
        cols = pl.ds(pl.multiple_of(h * HD, HD), HD)
        vt[h, pl.ds(0, HD), :] = vv[:, cols].T
        vt[h, pl.ds(HD, 16), :] = jnp.ones((16, 1024), BF)
        return carry

    lax.fori_loop(0, 6, turn, 0)
    swap_wait(0)
    swap_wait(3)

    arrive(gather(1, 0))
    start(gather(1, 1))
    arrive(gather(0, 2))
    start(gather(0, 3))
    arrive(gather(1, 1))
    start(gather(1, 2))
    x_wait(2)
    start(gather(2, 0))
    arrive(gather(0, 3))

    first = first_ref[0]

    def block(i):
        return jnp.bitwise_and(first + i, 15)

    def pieces(ref, i, cols):
        b, a = block(i - 1), block(i)
        return [ref[1, b // 4, jnp.bitwise_and(b, 3), :, cols], ref[0, a // 4, jnp.bitwise_and(a, 3), :, cols]]

    marks = pl.ds(768, HD)

    def audio_step(step, carry):
        half, tile = step // 5, lax.rem(step, 5)
        mark = jnp.concatenate(pieces(aq, 2 * tile, marks) + pieces(aq, 2 * tile + 1, marks), axis=0)
        tops, sums = [], []
        for hh in range(3):
            h = half * 3 + hh
            cols = pl.ds(pl.multiple_of(h * HD, HD), HD)
            q = jnp.concatenate(pieces(aq, 2 * tile, cols) + pieces(aq, 2 * tile + 1, cols), axis=0)
            q = jnp.concatenate([q, mark], axis=1)
            k = jnp.concatenate([vk[:, cols], ve[...]], axis=1)
            scores = lax.dot_general(k, q, (((1,), (1,)), ((), ())), preferred_element_type=F32) * SCALE
            top = jnp.maximum(jnp.max(scores, axis=0, keepdims=True), LOW).astype(BF).astype(F32)
            weights = jnp.exp2(scores - top).astype(BF)
            out = jnp.dot(vt[h], weights, preferred_element_type=F32)
            tops.append(top)
            sums.append(out[HD : HD + 1])
            for b in range(2):
                window[half, 2 * tile + b, pl.ds(hh * HD, HD), :] = out[:HD, b * HD : (b + 1) * HD].astype(BF)
        top, total = jnp.concatenate(tops, axis=0), jnp.concatenate(sums, axis=0)
        high = total.astype(BF).astype(F32)
        gap = jnp.zeros((1, 256), F32)
        stats = jnp.concatenate([top, gap, total - high, gap, high, jnp.zeros((5, 256), F32)], axis=0)
        for b in range(2):
            window[half, 2 * tile + b, pl.ds(STAT, 16), :] = stats[:, b * HD : (b + 1) * HD].astype(BF)

        @pl.when(step == 2)
        def _():
            arrive(gather(2, 0))
            start(gather(2, 1))

        @pl.when(step == 5)
        def _():
            arrive(gather(1, 2))
            start(gather(1, 3))
            arrive(gather(2, 1))
            start(gather(2, 2))

        return carry

    lax.fori_loop(0, 10, audio_step, 0)

    empty = jnp.where(lax.broadcasted_iota(jnp.int32, (16, HD), 0) < 3, LOW, 0.0)

    def place(b, carry):
        at = jnp.bitwise_and(b - first, 15)
        inside = (at < BLOCKS).astype(F32)
        at = jnp.minimum(at, BLOCKS - 1)
        bz, by = b // 4, lax.rem(b, 4)
        for half in range(2):
            body = window[half, at, pl.ds(0, STAT), :].astype(F32)
            part[half, bz, by, pl.ds(0, STAT), :] = (body * inside).astype(BF)
            stats = window[half, at, pl.ds(STAT, 16), :].astype(F32)
            part[half, bz, by, pl.ds(STAT, 16), :] = (stats * inside + empty * (1.0 - inside)).astype(BF)
        return carry

    lax.fori_loop(0, 16, place, 0)

    def slab(half, where, lo):
        if half == 0:
            return part.at[0, where, pl.ds(lo, 2)]
        return part.at[1, pl.ds(lo, 2), where]

    axes = ((z, zp, zm, z2, to_zp, to_zm), (y, yp, ym, y2, to_yp, to_ym))
    crosses = ((y, yp, ym, y2, to_yp, to_ym, to_y2), (z, zp, zm, z2, to_zp, to_zm, to_z2))

    def reduce1(half):
        _, p, m, two, to_p, to_m = axes[half]
        plan = (
            (slab(half, two, 0), to_p), (slab(half, two, 2), to_m),
            (slab(half, p, 2), to_p), (slab(half, m, 0), to_m),
            (slab(half, p, 0), to_p), (slab(half, m, 2), to_m),
        )
        return [
            remote(ref, got1.at[half, i], r_send.at[half, i], r_recv.at[half, i], dev)
            for i, (ref, dev) in enumerate(plan)
        ]

    def one(half, u):
        if half == 0:
            return part.at[0, z, u]
        return part.at[1, u, y]

    def reduce2(half):
        _, p, m, two, to_p, to_m, to_2 = crosses[half]
        return [
            remote(one(half, u), got2.at[half, i], r_send.at[half, 6 + i], r_recv.at[half, 6 + i], dev)
            for i, (u, dev) in enumerate(((p, to_p), (m, to_m), (two, to_2)))
        ]

    def merged(refs):
        stats = [ref[pl.ds(STAT, 16), :].astype(F32) for ref in refs]
        tops = [x[0:3] for x in stats]
        top = tops[0]
        for x in tops[1:]:
            top = jnp.maximum(top, x)
        factors = [jnp.exp2(x - top) for x in tops]
        total = sum((x[8:11] + x[4:7]) * f for x, f in zip(stats, factors))
        outs = [
            sum(ref[pl.ds(hh * HD, HD), :].astype(F32) * f[hh : hh + 1] for ref, f in zip(refs, factors))
            for hh in range(3)
        ]
        return outs, top, total

    def merge_into(target, sources):
        outs, top, total = merged([target] + sources)
        for hh in range(3):
            target[pl.ds(hh * HD, HD), :] = outs[hh].astype(BF)
        high = total.astype(BF).astype(F32)
        gap = jnp.zeros((1, HD), F32)
        stats = jnp.concatenate([top, gap, total - high, gap, high, jnp.zeros((5, HD), F32)], axis=0)
        target[pl.ds(STAT, 16), :] = stats.astype(BF)

    def merge_slab(half, where, lo, slots):
        def body(i, carry):
            target = part.at[0, where, lo + i] if half == 0 else part.at[1, lo + i, where]
            merge_into(target, [got1.at[half, slot, i] for slot in slots])
            return carry

        lax.fori_loop(0, 2, body, 0)

    def reduce_start(half):
        start(reduce1(half)[:4])

    def reduce_pass(half):
        _, p, m, *_ = axes[half]
        copies = reduce1(half)
        copies[0].wait_recv()
        merge_slab(half, p, 0, (0,))
        copies[4].start()
        copies[1].wait_recv()
        merge_slab(half, m, 2, (1,))
        copies[5].start()

    def reduce_cross(half):
        own = axes[half][0]
        arrive(reduce1(half)[2:])
        merge_slab(half, own, 0, (3, 4))
        merge_slab(half, own, 2, (2, 5))
        start(reduce2(half))

    def reduce_end(half):
        own = crosses[half][0]
        arrive(reduce2(half))
        outs, _, total = merged([one(half, own)] + [got2.at[half, i] for i in range(3)])
        scale = 1.0 / total
        for hh in range(3):
            done = (outs[hh] * scale[hh : hh + 1]).T
            ao[:, pl.ds((half * 3 + hh) * HD, HD)] = done.astype(BF)

    def results():
        mine = columns(core, 768)
        return [
            remote(ao.at[pl.ds(64, 64)], aout_hbm.at[:, mine], o_send.at[0], o_recv.at[core], result_low),
            remote(ao.at[pl.ds(0, 64)], aout_hbm.at[:, mine], o_send.at[1], o_recv.at[core], result_high),
        ]

    arrive(gather(2, 2))
    start(gather(2, 3))
    reduce_start(0)
    reduce_start(1)
    swap_wait(2)
    arrive(gather(1, 3))
    arrive(gather(2, 3))

    def video_step(h, carry):
        cols = pl.ds(pl.multiple_of(h * HD, HD), HD)

        def rows(ref, cc):
            return jnp.concatenate([piece for i in range(BLOCKS) for piece in pieces(ref, i, cc)], axis=0)

        k = jnp.concatenate([rows(ak, cols), rows(aq, marks)], axis=1)
        v = jnp.concatenate([rows(av, cols).T, jnp.ones((16, BLOCKS * HD), BF)], axis=0)
        for tile in range(4):
            here = pl.ds(tile * 256, 256)
            q = jnp.concatenate([vq[here, cols], ve[here, :]], axis=1)
            scores = lax.dot_general(k, q, (((1,), (1,)), ((), ())), preferred_element_type=F32) * SCALE
            top = jnp.max(scores, axis=0, keepdims=True)
            weights = jnp.exp2(scores - top).astype(BF)
            out = jnp.dot(v, weights, preferred_element_type=F32)
            done = out[:HD] * (1.0 / out[HD : HD + 1])
            vo[here, cols] = done.T.astype(BF)

        @pl.when(h == 0)
        def _():
            reduce_pass(0)
            reduce_pass(1)

        @pl.when(h == 2)
        def _():
            reduce_cross(0)
            reduce_cross(1)

        @pl.when(h == 4)
        def _():
            reduce_end(0)
            reduce_end(1)
            start(results())

        return carry

    lax.fori_loop(0, 6, video_step, 0)

    mine = columns(core, 768)
    away = remote(vo.at[other_rows], vout_hbm.at[:, mine], o_send.at[2], o_recv.at[2], other)
    here = pltpu.make_async_copy(vo.at[own_rows], vout_hbm.at[:, mine], o_local)
    away.start()
    here.start()

    for t in range(3):
        sent(x_step(t))
        for stage in range(4):
            sent(gather(t, stage))
    for i in range(4):
        swap(i)[0].wait_send()
    for half in range(2):
        sent(reduce1(half))
        sent(reduce2(half))
    sent(results())
    for cc in (0, 1):
        remote(
            ao.at[pl.ds(0, 64)], aout_hbm.at[:, pl.ds(cc * 768, 768)], o_send.at[0], o_recv.at[cc], result_low
        ).wait_recv()
    here.wait()
    away.wait()


def on_device(video_q, video_k, video_v, audio_q, audio_k, audio_v, video_clip, audio_clip):
    core = lax.rem(lax.axis_index("seq"), 2)
    video_mark, audio_mark = lax.rem(video_clip, CLIPS), lax.rem(audio_clip, CLIPS)
    lanes = jnp.arange(HD, dtype=jnp.int32)[None, :]
    video_extra = jnp.where(video_mark[:, None] == lanes, 0.0, FAR).astype(BF)
    audio_extra = (audio_mark[:, None] == lanes).astype(BF)
    audio_q = jnp.concatenate([audio_q[:, :768], audio_extra, audio_q[:, 768:], audio_extra], axis=1)
    first = jnp.where(core == 0, video_mark[0], video_mark[-1] - 1).reshape(1)
    anywhere = pl.BlockSpec(memory_space=pl.ANY)
    dma = pltpu.SemaphoreType.DMA
    return pl.pallas_call(
        kernel,
        out_shape=(
            jax.ShapeDtypeStruct(video_q.shape, BF),
            jax.ShapeDtypeStruct(audio_k.shape, BF),
        ),
        in_specs=[pl.BlockSpec(memory_space=pltpu.SMEM)] + [anywhere] * 7,
        out_specs=(anywhere, anywhere),
        scratch_shapes=[
            pltpu.VMEM((1024, 768), BF),
            pltpu.VMEM((1024, 768), BF),
            pltpu.VMEM((1024, 768), BF),
            pltpu.VMEM((1024, HD), BF),
            pltpu.VMEM((2, 4, 4, 64, 896), BF),
            pltpu.VMEM((2, 4, 4, 64, 768), BF),
            pltpu.VMEM((2, 4, 4, 64, 768), BF),
            pltpu.VMEM((6, HD + 16, 1024), BF),
            pltpu.VMEM((2, BLOCKS, ROWS, HD), BF),
            pltpu.VMEM((2, 4, 4, ROWS, HD), BF),
            pltpu.VMEM((2, 6, 2, ROWS, HD), BF),
            pltpu.VMEM((2, 3, ROWS, HD), BF),
            pltpu.VMEM((1024, 768), BF),
            pltpu.VMEM((HD, 768), BF),
            dma((3, 2)),
            dma((3, 2)),
            dma((3, 16)),
            dma((3, 16)),
            dma((4,)),
            dma((4,)),
            dma((4,)),
            dma((2, 9)),
            dma((2, 9)),
            dma((3,)),
            dma((3,)),
            dma,
        ],
        compiler_params=pltpu.CompilerParams(
            collective_id=0, has_side_effects=True, vmem_limit_bytes=56 * 1024 * 1024
        ),
    )(first, video_q, video_k, video_v, video_extra, audio_q, audio_k, audio_v)


def solution(mesh):
    spread = P(("grp", "seq"), None)
    return jax.shard_map(
        on_device,
        mesh=mesh,
        in_specs=(spread,) * 6 + (P(("grp", "seq")),) * 2,
        out_specs=(spread, spread),
        check_vma=False,
    )
```

time: 426 us -> 119 us (0.28)
  the two profiles are of different devices: /device:TPU:0 before, /device:TPU:1 now
where the time goes in v1:
time: 119 us
  Pallas kernels  109 us (92%)
  local copies, waits for them, and re-layouts  4.91 us (4%)
  other arithmetic  2.93 us (2%)
  between operations  1.96 us (2%)
    pallas_call x1, Pallas kernels, on_device(): pl.pallas_call(kernel, out_shape=(jax.ShapeDtypeStruct(video_q.shape, BF)...  109 us
    unnamed x4, local copies, waits for them, and re-layouts  3.37 us

profile of v1, /device:TPU:1, one launch (start us, length us, event | category | flops | bytes accessed | tf_op | source)
XLA Modules:
  0.0 119.0 jit_solution(947468935858007603)
XLA Ops:
  0.6 0.7 broadcast_remainder_fusion.1
  1.3 0.7 broadcast_remainder_fusion
  2.0 0.6 fusion.2
  3.9 0.1 fusion
  4.0 0.8 select_convert_fusion.ve_hbm
  4.7 1.0 fusion.1
  5.7 0.7 pad_maximum_fusion.aq_hbm
  6.4 109.2 %shard_map.95 = (bf16[512,1536]{1,0:T(8,128)(2,1)}, bf16[64,1536]{1,0:T(8,128)(2,1)}) custom-call(s32[1]{0:T(128)} %bitcast.2.first_ref, bf16[512,1536]{1,0:T(8,128)(2,1)} %vq_hbm.1, bf16[512,1536]{1,0:T(8,128)(2,1)} %vk_hbm.1, bf16[512,1536]{1,0:T(8,128)(2,1)} %vv_hbm.1, bf16[512,128]{1,0:T(8,128)(2,1)} %select_convert_fusion.ve_hbm, ...), custom_call_target="tpu_custom_call" | custom-call | tf_op jit(solution)/shard_map/pallas_call | solution.py:450
  115.6 0.0 copy-start
  115.6 2.7 %copy.12 = bf16[512,1536]{1,0:T(8,128)(2,1)} copy(bf16[512,1536]{1,0:T(8,128)(2,1)} %get-tuple-element.8) | data formatting | bytes 3145728
  118.3 0.0 copy-done
  118.3 0.7 copy.13
Async XLA Ops:
  115.6 2.7 %copy-start = (bf16[64,1536]{1,0:T(8,128)(2,1)S(1)}, bf16[64,1536]{1,0:T(8,128)(2,1)}, u32[]{:S(2)}) copy-start(bf16[64,1536]{1,0:T(8,128)(2,1)} %get-tuple-element.9) | copy-start | bytes 589828

commit v2 on v1

v2 whole, which is shorter than its diff:
```python
import math

import jax
import jax.numpy as jnp
from jax import lax
from jax.experimental import pallas as pl
from jax.experimental.pallas import tpu as pltpu
from jax.sharding import PartitionSpec as P

MESH = pl.DeviceIdType.MESH
BF = jnp.bfloat16
F32 = jnp.float32
HD = 128
CLIPS = 9
SCALE = math.log2(math.e) / math.sqrt(HD)
FAR = -1048576.0
LOW = -32768.0
BLOCKS = 10
STAT = 3 * HD
ROWS = STAT + 16


def kernel(
    clip_smem, video_clip, audio_clip, vq_hbm, vk_hbm, vv_hbm, aq_hbm, ak_hbm, av_hbm,
    vout_hbm, aout_hbm,
    vq, vk, vv, ve, aq, ak, av, mk, am, mk_own, vt, wt, buf_a, buf_b, tops, sums, window, part, got1, got2, vo, ao,
    x_send, x_recv, g_send, g_recv, v_send, v_recv, v_local, r_send, r_recv, o_send, o_recv, w_send, w_recv, w_local,
):
    g = lax.axis_index("grp")
    s = lax.axis_index("seq")
    core = lax.rem(s, 2)
    chip = s // 2
    z, y = chip // 4, lax.rem(chip, 4)
    zp, zm, z2 = lax.rem(z + 1, 4), lax.rem(z + 3, 4), lax.rem(z + 2, 4)
    yp, ym, y2 = lax.rem(y + 1, 4), lax.rem(y + 3, 4), lax.rem(y + 2, 4)
    gp, gm = lax.rem(g + 1, 4), lax.rem(g + 3, 4)

    def device(grp, zz, yy, cc):
        return (grp, (zz * 4 + yy) * 2 + cc)

    other = device(g, z, y, 1 - core)
    to_yp, to_ym, to_y2 = (device(g, z, b, core) for b in (yp, ym, y2))
    to_zp, to_zm, to_z2 = (device(g, b, y, core) for b in (zp, zm, z2))
    before = lax.rem(chip + 15, 16)
    after = lax.rem(chip + 1, 16)
    result_low = (gp, chip * 2)
    result_high = (gp, before * 2 + 1)

    barrier = pltpu.get_barrier_semaphore()

    def greet(dev):
        pl.semaphore_signal(barrier, inc=1, device_id=dev, device_id_type=MESH)

    for dev in (other, to_yp, to_ym, to_y2, to_zp, to_zm, to_z2):
        greet(dev)
    for cc in (0, 1):
        greet(device(gm, z, y, cc))
        greet(device(gp, z, y, cc))
    greet(result_high)

    @pl.when(core == 1)
    def _():
        greet((gm, after * 2))
        greet((gm, after * 2 + 1))

    pl.semaphore_wait(barrier, 12 + 2 * core)

    def remote(src, dst, ssem, rsem, dev):
        return pltpu.make_async_remote_copy(
            src_ref=src, dst_ref=dst, send_sem=ssem, recv_sem=rsem, device_id=dev, device_id_type=MESH
        )

    def columns(half, width):
        return pl.ds(pl.multiple_of(half * width, 128), width)

    tensors = ((aq_hbm, aq), (ak_hbm, ak), (av_hbm, av), (mk_own, mk))

    def x_copies(t, sender):
        src, dst = tensors[t]
        return [
            remote(
                src if t == 3 else src.at[:, pl.ds(cc * 768, 768)], dst.at[sender, z, y], x_send.at[t, cc],
                x_recv.at[t, sender], device(gm, z, y, cc),
            )
            for cc in (0, 1)
        ]

    def x_step(t):
        return x_copies(t, core)

    def x_wait(t):
        for cc in (0, 1):
            x_copies(t, cc)[0].wait_recv()

    def gather(t, stage):
        x = tensors[t][1]
        rows = x.shape[3] // 2
        low, high = pl.ds(0, rows), pl.ds(rows, rows)
        first, last = pl.ds(0, 2), pl.ds(2, 2)
        plan = (
            (x.at[0, z, y], to_yp),
            (x.at[0, z, y], to_ym),
            (x.at[1, z, y], to_zp),
            (x.at[1, z, y], to_zm),
        ), (
            (x.at[0, z, ym, low], to_yp),
            (x.at[0, z, yp, high], to_ym),
            (x.at[1, zm, y, low], to_zp),
            (x.at[1, zp, y, high], to_zm),
        ), (
            (x.at[0, z], to_zp),
            (x.at[0, z], to_zm),
            (x.at[1, :, y], to_yp),
            (x.at[1, :, y], to_ym),
        ), (
            (x.at[0, zm, first], to_zp),
            (x.at[0, zp, last], to_zm),
            (x.at[1, first, ym], to_yp),
            (x.at[1, last, yp], to_ym),
        )
        return [
            remote(ref, ref, g_send.at[t, stage * 4 + i], g_recv.at[t, stage * 4 + i], dev)
            for i, (ref, dev) in enumerate(plan[stage])
        ]

    def start(copies):
        for copy in copies:
            copy.start()

    def arrive(copies):
        for copy in copies:
            copy.wait_recv()

    def sent(copies):
        for copy in copies:
            copy.wait_send()

    video = ((vk_hbm, vk), (vv_hbm, vv), (vq_hbm, vq))
    own_rows = pl.ds(pl.multiple_of(core * 512, 512), 512)
    other_rows = pl.ds(pl.multiple_of((1 - core) * 512, 512), 512)

    def swap(i):
        src, dst = video[i]
        return (
            remote(src.at[:, columns(1 - core, 768)], dst.at[own_rows], v_send.at[i], v_recv.at[i], other),
            pltpu.make_async_copy(src.at[:, columns(core, 768)], dst.at[own_rows], v_local.at[i]),
        )

    def swap_start(i):
        away, here = swap(i)
        away.start()
        here.start()

    def swap_wait(i):
        away, here = swap(i)
        away.wait_recv()
        here.wait()

    def swap_marks():
        return remote(ve.at[own_rows], ve.at[own_rows], v_send.at[3], v_recv.at[3], other)

    start(x_step(0))
    swap_start(0)
    swap_start(1)

    numbers = (audio_clip[...] - gm * CLIPS).astype(F32)
    numbers = jnp.concatenate([numbers, numbers], axis=1)
    mk_own[...] = jnp.broadcast_to(numbers, (32, HD)).astype(BF)
    start(x_step(3))
    clips = lax.broadcasted_iota(jnp.int32, (HD, HD), 0)
    for i in range(4):
        same = video_clip[i : i + 1, :] - g * CLIPS == clips
        at = pl.multiple_of(core * 512 + i * HD, HD)
        ve[pl.ds(at, HD), :] = jnp.where(same, 0.0, FAR).T.astype(BF)
    swap_marks().start()

    x_wait(3)
    start(gather(3, 0))
    x_wait(0)
    start(gather(0, 0))
    start(x_step(1))
    arrive(gather(3, 0))
    start(gather(3, 1))
    arrive(gather(0, 0))
    start(gather(0, 1))
    arrive(gather(3, 1))
    start(gather(3, 2))
    arrive(gather(0, 1))
    start(gather(0, 2))
    x_wait(1)
    start(gather(1, 0))
    start(x_step(2))
    swap_start(2)

    swap_wait(1)

    def turn(h, carry):
        cols = pl.ds(pl.multiple_of(h * HD, HD), HD)
        vt[h, pl.ds(0, HD), :] = vv[:, cols].T
        vt[h, pl.ds(HD, 16), :] = jnp.ones((16, 1024), BF)
        return carry

    lax.fori_loop(0, 6, turn, 0)
    x_wait(2)
    start(gather(2, 0))
    arrive(gather(3, 2))
    start(gather(3, 3))
    arrive(gather(1, 0))
    start(gather(1, 1))
    arrive(gather(2, 0))
    start(gather(2, 1))
    arrive(gather(0, 2))
    start(gather(0, 3))
    arrive(gather(1, 1))
    start(gather(1, 2))
    arrive(gather(2, 1))
    start(gather(2, 2))
    arrive(gather(3, 3))

    lanes = lax.broadcasted_iota(jnp.int32, (HD, HD), 0).astype(F32)

    def expand(i, carry):
        bz, by = i // 4, lax.rem(i, 4)
        for cc in (0, 1):
            numbers = mk[cc, bz, by, pl.ds(0, 16), :].astype(F32)[0:1]
            am[cc, bz, by] = jnp.where(numbers == lanes, 1.0, 0.0).T[0:64].astype(BF)
        return carry

    lax.fori_loop(0, 16, expand, 0)
    swap_wait(0)
    swap_marks().wait_recv()
    arrive(gather(0, 3))

    first = jnp.where(core == 0, clip_smem[0], clip_smem[511] - 1) - g * CLIPS

    def block(i):
        return jnp.bitwise_and(first + i, 15)

    def pieces(ref, i, cols):
        b, a = block(i - 1), block(i)
        return [ref[1, b // 4, jnp.bitwise_and(b, 3), :, cols], ref[0, a // 4, jnp.bitwise_and(a, 3), :, cols]]

    marks = pl.ds(0, HD)

    def packed(top, total):
        high = total.astype(BF).astype(F32)
        gap = jnp.zeros((1, HD), F32)
        return jnp.concatenate([top, gap, total - high, gap, high, jnp.zeros((5, HD), F32)], axis=0)

    def pipeline(units, sizes, scores_of, finish, events):
        def both(u_scores, u_out, buf_scores, buf_out, top):
            q, k_of = scores_of(u_scores)
            if u_out is not None:
                top = jnp.max(top, axis=0, keepdims=True) * SCALE
                top, v_of, store = finish(u_out, top)
            high, total = None, None
            for c in range(sizes):
                rows = pl.ds(c * 256, 256)
                scores = lax.dot_general(k_of(c), q, (((1,), (1,)), ((), ())), preferred_element_type=F32)
                buf_scores[rows, :] = scores
                best = jnp.max(scores.reshape(32, 8, 256), axis=0)
                high = best if high is None else jnp.maximum(high, best)
                if u_out is not None:
                    weights = jnp.exp2(buf_out[rows, :] * SCALE - top).astype(BF)
                    out = jnp.dot(v_of(c), weights, preferred_element_type=F32)
                    total = out if total is None else total + out
            if u_out is not None:
                store(total, top)
            return high

        def body(i, top):
            u = 2 * i
            top = both(u + 1, u, buf_b, buf_a, top)
            top = both(jnp.minimum(u + 2, units - 1), u + 1, buf_a, buf_b, top)
            for at, event in events:
                pl.when(i == at)(event)
            return top

        lax.fori_loop(0, units // 2, body, both(0, None, buf_a, None, None))

    def audio_scores(u):
        h, tile = u // 5, lax.rem(u, 5)
        cols = pl.ds(pl.multiple_of(h * HD, HD), HD)
        mark = jnp.concatenate(pieces(am, 2 * tile, marks) + pieces(am, 2 * tile + 1, marks), axis=0)
        q = jnp.concatenate(pieces(aq, 2 * tile, cols) + pieces(aq, 2 * tile + 1, cols), axis=0)

        def k_of(c):
            rows = pl.ds(c * 256, 256)
            return jnp.concatenate([vk[rows, cols], ve[rows, :]], axis=1)

        return jnp.concatenate([q, mark], axis=1), k_of

    def audio_finish(u, top):
        h, tile = u // 5, lax.rem(u, 5)
        top = jnp.maximum(top, LOW).astype(BF).astype(F32)

        def v_of(c):
            return vt[h, :, pl.ds(c * 256, 256)]

        def store(out, top):
            where = pl.ds(pl.multiple_of(lax.rem(h, 3) * HD, HD), HD)
            for b in range(2):
                window[h // 3, 2 * tile + b, where, :] = out[:HD, b * HD : (b + 1) * HD].astype(BF)
                tops[h, 2 * tile + b] = jnp.broadcast_to(top[:, b * HD : (b + 1) * HD], (8, HD))
                sums[h, 2 * tile + b] = jnp.broadcast_to(out[HD : HD + 1, b * HD : (b + 1) * HD], (8, HD))

        return top, v_of, store

    empty = jnp.where(lax.broadcasted_iota(jnp.int32, (16, HD), 0) < 3, LOW, 0.0)

    def place(half, b):
        at = jnp.bitwise_and(b - first, 15)
        inside = (at < BLOCKS).astype(F32)
        at = jnp.minimum(at, BLOCKS - 1)
        bz, by = b // 4, lax.rem(b, 4)
        body = window[half, at, :, :].astype(F32)
        part[half, bz, by, pl.ds(0, STAT), :] = (body * inside).astype(BF)
        top = jnp.concatenate([tops[half * 3 + hh, at][0:1] for hh in range(3)], axis=0)
        total = jnp.concatenate([sums[half * 3 + hh, at][0:1] for hh in range(3)], axis=0)
        stats = packed(top, total)
        part[half, bz, by, pl.ds(STAT, 16), :] = (stats * inside + empty * (1.0 - inside)).astype(BF)

    def place_all(half):
        def body(b, carry):
            place(half, b)
            return carry

        lax.fori_loop(0, 16, body, 0)

    def slab(half, where, lo):
        if half == 0:
            return part.at[0, where, pl.ds(lo, 2)]
        return part.at[1, pl.ds(lo, 2), where]

    axes = ((z, zp, zm, z2, to_zp, to_zm), (y, yp, ym, y2, to_yp, to_ym))
    crosses = ((y, yp, ym, y2, to_yp, to_ym, to_y2), (z, zp, zm, z2, to_zp, to_zm, to_z2))

    def reduce1(half):
        _, p, m, two, to_p, to_m = axes[half]
        plan = (
            (slab(half, two, 0), to_p), (slab(half, two, 2), to_m),
            (slab(half, p, 2), to_p), (slab(half, m, 0), to_m),
            (slab(half, p, 0), to_p), (slab(half, m, 2), to_m),
        )
        return [
            remote(ref, got1.at[half, i], r_send.at[half, i], r_recv.at[half, i], dev)
            for i, (ref, dev) in enumerate(plan)
        ]

    def one(half, u):
        if half == 0:
            return part.at[0, z, u]
        return part.at[1, u, y]

    def reduce2(half):
        _, p, m, two, to_p, to_m, to_2 = crosses[half]
        return [
            remote(one(half, u), got2.at[half, i], r_send.at[half, 6 + i], r_recv.at[half, 6 + i], dev)
            for i, (u, dev) in enumerate(((p, to_p), (m, to_m), (two, to_2)))
        ]

    def merged(refs):
        stats = [ref[pl.ds(STAT, 16), :].astype(F32) for ref in refs]
        tops = [x[0:3] for x in stats]
        top = tops[0]
        for x in tops[1:]:
            top = jnp.maximum(top, x)
        factors = [jnp.exp2(x - top) for x in tops]
        total = sum((x[8:11] + x[4:7]) * f for x, f in zip(stats, factors))
        outs = [
            sum(ref[pl.ds(hh * HD, HD), :].astype(F32) * f[hh : hh + 1] for ref, f in zip(refs, factors))
            for hh in range(3)
        ]
        return outs, top, total

    def merge_into(target, sources):
        outs, top, total = merged([target] + sources)
        for hh in range(3):
            target[pl.ds(hh * HD, HD), :] = outs[hh].astype(BF)
        target[pl.ds(STAT, 16), :] = packed(top, total).astype(BF)

    def merge_slab(half, where, lo, slots):
        def body(i, carry):
            target = part.at[0, where, lo + i] if half == 0 else part.at[1, lo + i, where]
            merge_into(target, [got1.at[half, slot, i] for slot in slots])
            return carry

        lax.fori_loop(0, 2, body, 0)

    def reduce_start(half):
        start(reduce1(half)[:4])

    def reduce_pass(half):
        _, p, m, *_ = axes[half]
        copies = reduce1(half)
        copies[0].wait_recv()
        merge_slab(half, p, 0, (0,))
        copies[4].start()
        copies[1].wait_recv()
        merge_slab(half, m, 2, (1,))
        copies[5].start()

    def reduce_cross(half):
        own = axes[half][0]
        arrive(reduce1(half)[2:])
        merge_slab(half, own, 0, (3, 4))
        merge_slab(half, own, 2, (2, 5))
        start(reduce2(half))

    def reduce_end(half):
        own = crosses[half][0]
        arrive(reduce2(half))
        outs, _, total = merged([one(half, own)] + [got2.at[half, i] for i in range(3)])
        scale = 1.0 / total
        for hh in range(3):
            done = (outs[hh] * scale[hh : hh + 1]).T
            ao[:, pl.ds((half * 3 + hh) * HD, HD)] = done.astype(BF)

    def results(half):
        mine = pl.ds(pl.multiple_of(core * 768 + half * 384, 128), 384)
        cols = pl.ds(half * 384, 384)
        return [
            remote(
                ao.at[rows, cols], aout_hbm.at[:, mine], o_send.at[half, i], o_recv.at[half, core], dev
            )
            for i, (rows, dev) in enumerate(((pl.ds(64, 64), result_low), (pl.ds(0, 64), result_high)))
        ]

    def event_first():
        place_all(0)
        reduce_start(0)

    def event_k():
        arrive(gather(1, 2))
        start(gather(1, 3))

    def event_v():
        arrive(gather(2, 2))
        start(gather(2, 3))

    pipeline(30, 4, audio_scores, audio_finish, ((7, event_first), (9, event_k), (12, event_v)))
    place_all(1)
    reduce_start(1)
    reduce_pass(0)
    swap_wait(2)
    arrive(gather(1, 3))
    arrive(gather(2, 3))

    def turn_window(h, carry):
        cols = pl.ds(pl.multiple_of(h * HD, HD), HD)
        for i in range(BLOCKS):
            wt[h, pl.ds(0, HD), pl.ds(i * HD, HD)] = jnp.concatenate(pieces(av, i, cols), axis=0).T
        wt[h, pl.ds(HD, 16), :] = jnp.ones((16, BLOCKS * HD), BF)
        return carry

    lax.fori_loop(0, 6, turn_window, 0)

    def video_scores(u):
        h, tile = u // 4, lax.rem(u, 4)
        cols = pl.ds(pl.multiple_of(h * HD, HD), HD)
        here = pl.ds(pl.multiple_of(tile * 256, 256), 256)

        def k_of(c):
            k = pieces(ak, 2 * c, cols) + pieces(ak, 2 * c + 1, cols)
            mark = pieces(am, 2 * c, marks) + pieces(am, 2 * c + 1, marks)
            return jnp.concatenate([jnp.concatenate(k, axis=0), jnp.concatenate(mark, axis=0)], axis=1)

        return jnp.concatenate([vq[here, cols], ve[here, :]], axis=1), k_of

    def video_finish(u, top):
        h, tile = u // 4, lax.rem(u, 4)
        cols = pl.ds(pl.multiple_of(h * HD, HD), HD)
        here = pl.ds(pl.multiple_of(tile * 256, 256), 256)

        def v_of(c):
            return wt[h, :, pl.ds(c * 256, 256)]

        def store(out, top):
            done = out[:HD] * (1.0 / out[HD : HD + 1])
            vo[here, cols] = done.T.astype(BF)

        return top, v_of, store

    def video_copies(i):
        cols = pl.ds(i * 256, 256)
        mine = pl.ds(pl.multiple_of(core * 768 + i * 256, 128), 256)
        return (
            remote(vo.at[other_rows, cols], vout_hbm.at[:, mine], w_send.at[i], w_recv.at[i], other),
            pltpu.make_async_copy(vo.at[own_rows, cols], vout_hbm.at[:, mine], w_local.at[i]),
        )

    def event_pass():
        reduce_pass(1)

    def event_cross0():
        reduce_cross(0)

    def event_cross1():
        reduce_cross(1)
        start(video_copies(0))

    def event_end0():
        reduce_end(0)
        start(results(0))

    def event_end1():
        reduce_end(1)
        start(results(1))
        start(video_copies(1))

    pipeline(
        24, 5, video_scores, video_finish,
        ((0, event_pass), (2, event_cross0), (4, event_cross1), (6, event_end0), (8, event_end1)),
    )
    start(video_copies(2))

    for t in range(4):
        sent(x_step(t))
        for stage in range(4):
            sent(gather(t, stage))
    for i in range(3):
        swap(i)[0].wait_send()
    swap_marks().wait_send()
    for half in range(2):
        sent(reduce1(half))
        sent(reduce2(half))
        sent(results(half))
        for cc in (0, 1):
            mine = pl.ds(cc * 768 + half * 384, 384)
            remote(
                ao.at[pl.ds(0, 64), pl.ds(half * 384, 384)], aout_hbm.at[:, mine], o_send.at[half, 0],
                o_recv.at[half, cc], result_low,
            ).wait_recv()
    for i in range(3):
        away, here = video_copies(i)
        here.wait()
        away.wait()


def on_device(video_q, video_k, video_v, audio_q, audio_k, audio_v, video_clip, audio_clip):
    anywhere = pl.BlockSpec(memory_space=pl.ANY)
    dma = pltpu.SemaphoreType.DMA
    return pl.pallas_call(
        kernel,
        out_shape=(
            jax.ShapeDtypeStruct(video_q.shape, BF),
            jax.ShapeDtypeStruct(audio_k.shape, BF),
        ),
        in_specs=[
            pl.BlockSpec(memory_space=pltpu.SMEM),
            pl.BlockSpec(memory_space=pltpu.VMEM),
            pl.BlockSpec(memory_space=pltpu.VMEM),
        ]
        + [anywhere] * 6,
        out_specs=(anywhere, anywhere),
        scratch_shapes=[
            pltpu.VMEM((1024, 768), BF),
            pltpu.VMEM((1024, 768), BF),
            pltpu.VMEM((1024, 768), BF),
            pltpu.VMEM((1024, HD), BF),
            pltpu.VMEM((2, 4, 4, 64, 768), BF),
            pltpu.VMEM((2, 4, 4, 64, 768), BF),
            pltpu.VMEM((2, 4, 4, 64, 768), BF),
            pltpu.VMEM((2, 4, 4, 32, HD), BF),
            pltpu.VMEM((2, 4, 4, 64, HD), BF),
            pltpu.VMEM((32, HD), BF),
            pltpu.VMEM((6, HD + 16, 1024), BF),
            pltpu.VMEM((6, HD + 16, BLOCKS * HD), BF),
            pltpu.VMEM((BLOCKS * HD, 256), F32),
            pltpu.VMEM((BLOCKS * HD, 256), F32),
            pltpu.VMEM((6, BLOCKS, 8, HD), F32),
            pltpu.VMEM((6, BLOCKS, 8, HD), F32),
            pltpu.VMEM((2, BLOCKS, STAT, HD), BF),
            pltpu.VMEM((2, 4, 4, ROWS, HD), BF),
            pltpu.VMEM((2, 6, 2, ROWS, HD), BF),
            pltpu.VMEM((2, 3, ROWS, HD), BF),
            pltpu.VMEM((1024, 768), BF),
            pltpu.VMEM((HD, 768), BF),
            dma((4, 2)),
            dma((4, 2)),
            dma((4, 16)),
            dma((4, 16)),
            dma((4,)),
            dma((4,)),
            dma((3,)),
            dma((2, 9)),
            dma((2, 9)),
            dma((2, 2)),
            dma((2, 2)),
            dma((3,)),
            dma((3,)),
            dma((3,)),
        ],
        compiler_params=pltpu.CompilerParams(
            collective_id=0, has_side_effects=True, vmem_limit_bytes=56 * 1024 * 1024
        ),
    )(
        video_clip, video_clip.reshape(4, HD), audio_clip.reshape(1, 64), video_q, video_k, video_v, audio_q, audio_k,
        audio_v,
    )


def solution(mesh):
    spread = P(("grp", "seq"), None)
    return jax.shard_map(
        on_device,
        mesh=mesh,
        in_specs=(spread,) * 6 + (P(("grp", "seq")),) * 2,
        out_specs=(spread, spread),
        check_vma=False,
    )
```

time: 119 us -> 107 us (0.90)
  Pallas kernels: 109 us -> 103 us
  other arithmetic: 2.93 us -> 0 us
  local copies, waits for them, and re-layouts: 4.91 us -> 3.37 us
  between operations: 1.96 us -> 0.65 us
    pallas_call x1, Pallas kernels: 109 us -> 103 us  [on_device(): pl.pallas_call(kernel, out_shape=(jax.ShapeDtypeStruct(video_q.shape, BF)...]
    slice x2 -> x0, local copies, waits for them, and re-layouts: 1.54 us -> none  [the longest x1 0.95 us: on_device(): audio_q[:, :768]]
    rem x2 -> x0, other arithmetic: 1.36 us -> none  [the longest x1 0.69 us: on_device(): lax.rem(video_clip, CLIPS)]
where the time goes in v2:
time: 107 us
  Pallas kernels  103 us (96%)
  local copies, waits for them, and re-layouts  3.37 us (3%)
    pallas_call x1, Pallas kernels, on_device(): pl.pallas_call(kernel, out_shape=(jax.ShapeDtypeStruct(video_q.shape, BF)...  103 us
    unnamed x4, local copies, waits for them, and re-layouts  3.37 us

profile of v2, /device:TPU:1, one launch (start us, length us, event | category | flops | bytes accessed | tf_op | source)
XLA Modules:
  0.0 106.5 jit_solution(10910043096728300739)
XLA Ops:
  0.6 102.5 %shard_map.95 = (bf16[512,1536]{1,0:T(8,128)(2,1)}, bf16[64,1536]{1,0:T(8,128)(2,1)}) custom-call(s32[512]{0:T(512)} %clip_smem.1, s32[4,128]{1,0:T(4,128)} %bitcast.2, s32[1,64]{1,0:T(1,128)} %bitcast.3, bf16[512,1536]{1,0:T(8,128)(2,1)} %vq_hbm.1, bf16[512,1536]{1,0:T(8,128)(2,1)} %vk_hbm.1, bf16[512,1536]{1,0:T(8,128)(2,1)} %vv_hbm.1, ...), custom_call_target="tpu_custom_call" | custom-call | tf_op jit(solution)/shard_map/pallas_call | solution.py:543
  103.2 0.0 copy-start
  103.2 2.7 %copy.12 = bf16[512,1536]{1,0:T(8,128)(2,1)} copy(bf16[512,1536]{1,0:T(8,128)(2,1)} %get-tuple-element.4) | data formatting | bytes 3145728
  105.9 0.0 copy-done
  105.9 0.7 copy.13
Async XLA Ops:
  103.2 2.7 %copy-start = (bf16[64,1536]{1,0:T(8,128)(2,1)S(1)}, bf16[64,1536]{1,0:T(8,128)(2,1)}, u32[]{:S(2)}) copy-start(bf16[64,1536]{1,0:T(8,128)(2,1)} %get-tuple-element.5) | copy-start | bytes 589828

commit v3 on v2

--- a/solution.py
+++ b/solution.py
@@ -39,8 +39,8 @@
         return (grp, (zz * 4 + yy) * 2 + cc)
 
     other = device(g, z, y, 1 - core)
-    to_yp, to_ym, to_y2 = (device(g, z, b, core) for b in (yp, ym, y2))
-    to_zp, to_zm, to_z2 = (device(g, b, y, core) for b in (zp, zm, z2))
+    to_yp, to_ym = (device(g, z, b, core) for b in (yp, ym))
+    to_zp, to_zm = (device(g, b, y, core) for b in (zp, zm))
     before = lax.rem(chip + 15, 16)
     after = lax.rem(chip + 1, 16)
     result_low = (gp, chip * 2)
@@ -51,7 +51,7 @@
     def greet(dev):
         pl.semaphore_signal(barrier, inc=1, device_id=dev, device_id_type=MESH)
 
-    for dev in (other, to_yp, to_ym, to_y2, to_zp, to_zm, to_z2):
+    for dev in (other, to_yp, to_ym, to_zp, to_zm):
         greet(dev)
     for cc in (0, 1):
         greet(device(gm, z, y, cc))
@@ -63,7 +63,7 @@
         greet((gm, after * 2))
         greet((gm, after * 2 + 1))
 
-    pl.semaphore_wait(barrier, 12 + 2 * core)
+    pl.semaphore_wait(barrier, 10 + 2 * core)
 
     def remote(src, dst, ssem, rsem, dev):
         return pltpu.make_async_remote_copy(
@@ -256,7 +256,7 @@
             high, total = None, None
             for c in range(sizes):
                 rows = pl.ds(c * 256, 256)
-                scores = lax.dot_general(k_of(c), q, (((1,), (1,)), ((), ())), preferred_element_type=F32)
+                scores = jnp.dot(k_of(c), q, preferred_element_type=F32)
                 buf_scores[rows, :] = scores
                 best = jnp.max(scores.reshape(32, 8, 256), axis=0)
                 high = best if high is None else jnp.maximum(high, best)
@@ -288,7 +288,7 @@
             rows = pl.ds(c * 256, 256)
             return jnp.concatenate([vk[rows, cols], ve[rows, :]], axis=1)
 
-        return jnp.concatenate([q, mark], axis=1), k_of
+        return jnp.concatenate([q, mark], axis=1).T, k_of
 
     def audio_finish(u, top):
         h, tile = u // 5, lax.rem(u, 5)
@@ -333,7 +333,13 @@
         return part.at[1, pl.ds(lo, 2), where]
 
     axes = ((z, zp, zm, z2, to_zp, to_zm), (y, yp, ym, y2, to_yp, to_ym))
-    crosses = ((y, yp, ym, y2, to_yp, to_ym, to_y2), (z, zp, zm, z2, to_zp, to_zm, to_z2))
+    turn_by = 1 + 2 * core
+
+    def cross(at, two):
+        p, m = lax.rem(at + turn_by, 4), lax.rem(at + 4 - turn_by, 4)
+        return at, p, m, two
+
+    crosses = (cross(y, y2), cross(z, z2))
 
     def reduce1(half):
         _, p, m, two, to_p, to_m = axes[half]
@@ -353,10 +359,11 @@
         return part.at[1, u, y]
 
     def reduce2(half):
-        _, p, m, two, to_p, to_m, to_2 = crosses[half]
+        _, p, m, two = crosses[half]
+        to_p, to_m = (device(g, z, u, core) if half == 0 else device(g, u, y, core) for u in (p, m))
         return [
             remote(one(half, u), got2.at[half, i], r_send.at[half, 6 + i], r_recv.at[half, 6 + i], dev)
-            for i, (u, dev) in enumerate(((p, to_p), (m, to_m), (two, to_2)))
+            for i, (u, dev) in enumerate(((two, to_p), (m, to_m), (p, to_p)))
         ]
 
     def merged(refs):
@@ -405,12 +412,18 @@
         arrive(reduce1(half)[2:])
         merge_slab(half, own, 0, (3, 4))
         merge_slab(half, own, 2, (2, 5))
-        start(reduce2(half))
+        start(reduce2(half)[:2])
+
+    def reduce_cross_pass(half):
+        copies = reduce2(half)
+        copies[0].wait_recv()
+        merge_into(one(half, crosses[half][1]), [got2.at[half, 0]])
+        copies[2].start()
 
     def reduce_end(half):
         own = crosses[half][0]
-        arrive(reduce2(half))
-        outs, _, total = merged([one(half, own)] + [got2.at[half, i] for i in range(3)])
+        arrive(reduce2(half)[1:])
+        outs, _, total = merged([one(half, own)] + [got2.at[half, i] for i in (1, 2)])
         scale = 1.0 / total
         for hh in range(3):
             done = (outs[hh] * scale[hh : hh + 1]).T
@@ -465,7 +478,7 @@
             mark = pieces(am, 2 * c, marks) + pieces(am, 2 * c + 1, marks)
             return jnp.concatenate([jnp.concatenate(k, axis=0), jnp.concatenate(mark, axis=0)], axis=1)
 
-        return jnp.concatenate([vq[here, cols], ve[here, :]], axis=1), k_of
+        return jnp.concatenate([vq[here, cols], ve[here, :]], axis=1).T, k_of
 
     def video_finish(u, top):
         h, tile = u // 4, lax.rem(u, 4)
@@ -496,12 +509,14 @@
         reduce_cross(0)
 
     def event_cross1():
+        reduce_cross_pass(0)
         reduce_cross(1)
         start(video_copies(0))
 
     def event_end0():
         reduce_end(0)
         start(results(0))
+        reduce_cross_pass(1)
 
     def event_end1():
         reduce_end(1)

time: 107 us -> 110 us (1.028)
  Pallas kernels: 103 us -> 105 us
    pallas_call x1, Pallas kernels: 103 us -> 105 us  [on_device(): pl.pallas_call(kernel, out_shape=(jax.ShapeDtypeStruct(video_q.shape, BF)...]
where the time goes in v3:
time: 110 us; the launch traced here: 109 us
  Pallas kernels  105 us (95%)
  local copies, waits for them, and re-layouts  3.37 us (3%)
    pallas_call x1, Pallas kernels, on_device(): pl.pallas_call(kernel, out_shape=(jax.ShapeDtypeStruct(video_q.shape, BF)...  105 us
    unnamed x4, local copies, waits for them, and re-layouts  3.37 us

profile of v3, /device:TPU:1, one launch (start us, length us, event | category | flops | bytes accessed | tf_op | source)
XLA Modules:
  0.0 109.4 jit_solution(18136067199765859811)
XLA Ops:
  0.6 105.4 %shard_map.95 = (bf16[512,1536]{1,0:T(8,128)(2,1)}, bf16[64,1536]{1,0:T(8,128)(2,1)}) custom-call(s32[512]{0:T(512)} %clip_smem.1, s32[4,128]{1,0:T(4,128)} %bitcast.2, s32[1,64]{1,0:T(1,128)} %bitcast.3, bf16[512,1536]{1,0:T(8,128)(2,1)} %vq_hbm.1, bf16[512,1536]{1,0:T(8,128)(2,1)} %vk_hbm.1, bf16[512,1536]{1,0:T(8,128)(2,1)} %vv_hbm.1, ...), custom_call_target="tpu_custom_call" | custom-call | tf_op jit(solution)/shard_map/pallas_call | solution.py:558
  106.1 0.0 copy-start
  106.1 2.7 %copy.12 = bf16[512,1536]{1,0:T(8,128)(2,1)} copy(bf16[512,1536]{1,0:T(8,128)(2,1)} %get-tuple-element.4) | data formatting | bytes 3145728
  108.8 0.0 copy-done
  108.8 0.7 copy.13
Async XLA Ops:
  106.1 2.7 %copy-start = (bf16[64,1536]{1,0:T(8,128)(2,1)S(1)}, bf16[64,1536]{1,0:T(8,128)(2,1)}, u32[]{:S(2)}) copy-start(bf16[64,1536]{1,0:T(8,128)(2,1)} %get-tuple-element.5) | copy-start | bytes 589828

commit v4 on v3

--- a/solution.py
+++ b/solution.py
@@ -20,10 +20,20 @@
 ROWS = STAT + 16
 
 
+ORDER = (
+    "1Q", "2Q", "3Q", "vqs", "xKs", "xVs", "1K", "1V", "4Q", "ex", "2K", "vt", "2V", "3K",
+    "A", 2, "3V", 8, "4K", 12, "p0", 13, "r1_0",
+    "B", "p1", "r1_1",
+    "X", 3, "4V", 5, "r2_0", "r2_1",
+    "T", "tw", "ca_0", "ca_1",
+    "Y", 1, "cb_0", "cb_1", "w0", 2, "o_0", 3, "o_1", "w1", 5, "w2",
+)
+
+
 def kernel(
     clip_smem, video_clip, audio_clip, vq_hbm, vk_hbm, vv_hbm, aq_hbm, ak_hbm, av_hbm,
     vout_hbm, aout_hbm,
-    vq, vk, vv, ve, aq, ak, av, mk, am, mk_own, vt, wt, buf_a, buf_b, tops, sums, window, part, got1, got2, vo, ao,
+    vq, vk, vv, ve, aq, ak, av, mk, am, mk_own, vt, buf_c, buf_d, buf_a, buf_b, wb, tops, sums, window, part, got1, got2, vo, ao,
     x_send, x_recv, g_send, g_recv, v_send, v_recv, v_local, r_send, r_recv, o_send, o_recv, w_send, w_recv, w_local,
 ):
     g = lax.axis_index("grp")
@@ -88,7 +98,12 @@
     def x_step(t):
         return x_copies(t, core)
 
+    here_already = set()
+
     def x_wait(t):
+        if t in here_already:
+            return
+        here_already.add(t)
         for cc in (0, 1):
             x_copies(t, cc)[0].wait_recv()
 
@@ -174,50 +189,13 @@
         ve[pl.ds(at, HD), :] = jnp.where(same, 0.0, FAR).T.astype(BF)
     swap_marks().start()
 
-    x_wait(3)
-    start(gather(3, 0))
-    x_wait(0)
-    start(gather(0, 0))
-    start(x_step(1))
-    arrive(gather(3, 0))
-    start(gather(3, 1))
-    arrive(gather(0, 0))
-    start(gather(0, 1))
-    arrive(gather(3, 1))
-    start(gather(3, 2))
-    arrive(gather(0, 1))
-    start(gather(0, 2))
-    x_wait(1)
-    start(gather(1, 0))
-    start(x_step(2))
-    swap_start(2)
-
-    swap_wait(1)
-
     def turn(h, carry):
         cols = pl.ds(pl.multiple_of(h * HD, HD), HD)
         vt[h, pl.ds(0, HD), :] = vv[:, cols].T
         vt[h, pl.ds(HD, 16), :] = jnp.ones((16, 1024), BF)
         return carry
 
-    lax.fori_loop(0, 6, turn, 0)
-    x_wait(2)
-    start(gather(2, 0))
-    arrive(gather(3, 2))
-    start(gather(3, 3))
-    arrive(gather(1, 0))
-    start(gather(1, 1))
-    arrive(gather(2, 0))
-    start(gather(2, 1))
-    arrive(gather(0, 2))
-    start(gather(0, 3))
-    arrive(gather(1, 1))
-    start(gather(1, 2))
-    arrive(gather(2, 1))
-    start(gather(2, 2))
-    arrive(gather(3, 3))
-
-    lanes = lax.broadcasted_iota(jnp.int32, (HD, HD), 0).astype(F32)
+    lanes = clips.astype(F32)
 
     def expand(i, carry):
         bz, by = i // 4, lax.rem(i, 4)
@@ -226,11 +204,6 @@
             am[cc, bz, by] = jnp.where(numbers == lanes, 1.0, 0.0).T[0:64].astype(BF)
         return carry
 
-    lax.fori_loop(0, 16, expand, 0)
-    swap_wait(0)
-    swap_marks().wait_recv()
-    arrive(gather(0, 3))
-
     first = jnp.where(core == 0, clip_smem[0], clip_smem[511] - 1) - g * CLIPS
 
     def block(i):
@@ -247,36 +220,46 @@
         gap = jnp.zeros((1, HD), F32)
         return jnp.concatenate([top, gap, total - high, gap, high, jnp.zeros((5, HD), F32)], axis=0)
 
+    def run_events(i, events):
+        for at in sorted({at for at, _ in events}):
+
+            @pl.when(i == at)
+            def _():
+                for where, event in events:
+                    if where == at:
+                        event()
+
     def pipeline(units, sizes, scores_of, finish, events):
         def both(u_scores, u_out, buf_scores, buf_out, top):
             q, k_of = scores_of(u_scores)
+            store = None
             if u_out is not None:
                 top = jnp.max(top, axis=0, keepdims=True) * SCALE
-                top, v_of, store = finish(u_out, top)
+                top, use, store = finish(u_out, top)
             high, total = None, None
             for c in range(sizes):
                 rows = pl.ds(c * 256, 256)
-                scores = jnp.dot(k_of(c), q, preferred_element_type=F32)
+                scores = lax.dot_general(k_of(c), q, (((1,), (1,)), ((), ())), preferred_element_type=F32)
                 buf_scores[rows, :] = scores
                 best = jnp.max(scores.reshape(32, 8, 256), axis=0)
                 high = best if high is None else jnp.maximum(high, best)
                 if u_out is not None:
                     weights = jnp.exp2(buf_out[rows, :] * SCALE - top).astype(BF)
-                    out = jnp.dot(v_of(c), weights, preferred_element_type=F32)
-                    total = out if total is None else total + out
-            if u_out is not None:
+                    out = use(c, weights)
+                    if store is not None:
+                        total = out if total is None else total + out
+            if store is not None:
                 store(total, top)
             return high
 
         def body(i, top):
             u = 2 * i
-            top = both(u + 1, u, buf_b, buf_a, top)
-            top = both(jnp.minimum(u + 2, units - 1), u + 1, buf_a, buf_b, top)
-            for at, event in events:
-                pl.when(i == at)(event)
+            top = both(u + 1, u, buf_d, buf_c, top)
+            top = both(jnp.minimum(u + 2, units - 1), u + 1, buf_c, buf_d, top)
+            run_events(i, events)
             return top
 
-        lax.fori_loop(0, units // 2, body, both(0, None, buf_a, None, None))
+        lax.fori_loop(0, units // 2, body, both(0, None, buf_c, None, None))
 
     def audio_scores(u):
         h, tile = u // 5, lax.rem(u, 5)
@@ -288,14 +271,14 @@
             rows = pl.ds(c * 256, 256)
             return jnp.concatenate([vk[rows, cols], ve[rows, :]], axis=1)
 
-        return jnp.concatenate([q, mark], axis=1).T, k_of
+        return jnp.concatenate([q, mark], axis=1), k_of
 
     def audio_finish(u, top):
         h, tile = u // 5, lax.rem(u, 5)
         top = jnp.maximum(top, LOW).astype(BF).astype(F32)
 
-        def v_of(c):
-            return vt[h, :, pl.ds(c * 256, 256)]
+        def use(c, weights):
+            return jnp.dot(vt[h, :, pl.ds(c * 256, 256)], weights, preferred_element_type=F32)
 
         def store(out, top):
             where = pl.ds(pl.multiple_of(lax.rem(h, 3) * HD, HD), HD)
@@ -304,11 +287,11 @@
                 tops[h, 2 * tile + b] = jnp.broadcast_to(top[:, b * HD : (b + 1) * HD], (8, HD))
                 sums[h, 2 * tile + b] = jnp.broadcast_to(out[HD : HD + 1, b * HD : (b + 1) * HD], (8, HD))
 
-        return top, v_of, store
+        return top, use, store
 
     empty = jnp.where(lax.broadcasted_iota(jnp.int32, (16, HD), 0) < 3, LOW, 0.0)
 
-    def place(half, b):
+    def place_block(half, b):
         at = jnp.bitwise_and(b - first, 15)
         inside = (at < BLOCKS).astype(F32)
         at = jnp.minimum(at, BLOCKS - 1)
@@ -322,7 +305,7 @@
 
     def place_all(half):
         def body(b, carry):
-            place(half, b)
+            place_block(half, b)
             return carry
 
         lax.fori_loop(0, 16, body, 0)
@@ -439,60 +422,52 @@
             for i, (rows, dev) in enumerate(((pl.ds(64, 64), result_low), (pl.ds(0, 64), result_high)))
         ]
 
-    def event_first():
-        place_all(0)
-        reduce_start(0)
-
-    def event_k():
-        arrive(gather(1, 2))
-        start(gather(1, 3))
-
-    def event_v():
-        arrive(gather(2, 2))
-        start(gather(2, 3))
-
-    pipeline(30, 4, audio_scores, audio_finish, ((7, event_first), (9, event_k), (12, event_v)))
-    place_all(1)
-    reduce_start(1)
-    reduce_pass(0)
-    swap_wait(2)
-    arrive(gather(1, 3))
-    arrive(gather(2, 3))
-
-    def turn_window(h, carry):
-        cols = pl.ds(pl.multiple_of(h * HD, HD), HD)
-        for i in range(BLOCKS):
-            wt[h, pl.ds(0, HD), pl.ds(i * HD, HD)] = jnp.concatenate(pieces(av, i, cols), axis=0).T
-        wt[h, pl.ds(HD, 16), :] = jnp.ones((16, BLOCKS * HD), BF)
-        return carry
-
-    lax.fori_loop(0, 6, turn_window, 0)
-
-    def video_scores(u):
-        h, tile = u // 4, lax.rem(u, 4)
-        cols = pl.ds(pl.multiple_of(h * HD, HD), HD)
-        here = pl.ds(pl.multiple_of(tile * 256, 256), 256)
-
-        def k_of(c):
-            k = pieces(ak, 2 * c, cols) + pieces(ak, 2 * c + 1, cols)
-            mark = pieces(am, 2 * c, marks) + pieces(am, 2 * c + 1, marks)
-            return jnp.concatenate([jnp.concatenate(k, axis=0), jnp.concatenate(mark, axis=0)], axis=1)
-
-        return jnp.concatenate([vq[here, cols], ve[here, :]], axis=1).T, k_of
-
-    def video_finish(u, top):
-        h, tile = u // 4, lax.rem(u, 4)
-        cols = pl.ds(pl.multiple_of(h * HD, HD), HD)
-        here = pl.ds(pl.multiple_of(tile * 256, 256), 256)
-
-        def v_of(c):
-            return wt[h, :, pl.ds(c * 256, 256)]
-
-        def store(out, top):
-            done = out[:HD] * (1.0 / out[HD : HD + 1])
-            vo[here, cols] = done.T.astype(BF)
-
-        return top, v_of, store
+    def rows_of(ref, i, cols):
+        return jnp.concatenate(pieces(ref, 2 * i, cols) + pieces(ref, 2 * i + 1, cols), axis=0)
+
+    def video_unit(u):
+        cols = pl.ds(pl.multiple_of(u // 2 * HD, HD), HD)
+        return cols, pl.ds(pl.multiple_of(lax.rem(u, 2) * 512, 512), 512)
+
+    def video_both(u_scores, u_out, buf_scores, buf_out):
+        cols, here = video_unit(u_scores)
+        q = jnp.concatenate([vq[here, cols], ve[here, :]], axis=1)
+        row = 0
+        for c in range(5):
+            k = jnp.concatenate([rows_of(ak, c, cols), rows_of(am, c, marks)], axis=1)
+            buf_scores[:, c * 256 : (c + 1) * 256] = lax.dot_general(
+                q, k, (((1,), (1,)), ((), ())), preferred_element_type=F32
+            )
+            if u_out is not None:
+                for _ in range(7 if c < 2 else 6):
+                    scores = buf_out[row : row + 16, :]
+                    top = jnp.max(scores, axis=1, keepdims=True) * SCALE
+                    wb[u_out, row : row + 16, :] = jnp.exp2(scores * SCALE - top).astype(BF)
+                    row += 16
+
+    def video_weights(events):
+        def body(i, carry):
+            u = 2 * i
+            video_both(u + 1, u, buf_b, buf_a)
+            video_both(jnp.minimum(u + 2, 11), u + 1, buf_a, buf_b)
+            run_events(i, events)
+            return carry
+
+        video_both(0, None, buf_a, None)
+        lax.fori_loop(0, 6, body, 0)
+
+    def video_values(events):
+        def body(i, carry):
+            cols, _ = video_unit(2 * i)
+            v = jnp.concatenate([rows_of(av, c, cols) for c in range(5)], axis=0)
+            v = jnp.concatenate([v, jnp.ones((BLOCKS * HD, HD), BF)], axis=1)
+            for j in range(2):
+                out = jnp.dot(wb[2 * i + j], v, preferred_element_type=F32)
+                vo[pl.ds(j * 512, 512), cols] = (out[:, :HD] / out[:, HD:]).astype(BF)
+            run_events(i, events)
+            return carry
+
+        lax.fori_loop(0, 6, body, 0)
 
     def video_copies(i):
         cols = pl.ds(i * 256, 256)
@@ -502,32 +477,80 @@
             pltpu.make_async_copy(vo.at[own_rows, cols], vout_hbm.at[:, mine], w_local.at[i]),
         )
 
-    def event_pass():
-        reduce_pass(1)
-
-    def event_cross0():
-        reduce_cross(0)
-
-    def event_cross1():
-        reduce_cross_pass(0)
-        reduce_cross(1)
-        start(video_copies(0))
-
-    def event_end0():
-        reduce_end(0)
-        start(results(0))
-        reduce_cross_pass(1)
-
-    def event_end1():
-        reduce_end(1)
-        start(results(1))
-        start(video_copies(1))
-
-    pipeline(
-        24, 5, video_scores, video_finish,
-        ((0, event_pass), (2, event_cross0), (4, event_cross1), (6, event_end0), (8, event_end1)),
-    )
-    start(video_copies(2))
+    def take(t, stage):
+        for tensor in (3, 0) if t == 0 else (t,):
+            if stage == 0:
+                x_wait(tensor)
+            else:
+                arrive(gather(tensor, stage - 1))
+            start(gather(tensor, stage))
+
+    def x_next(t):
+        x_wait(t - 1)
+        start(x_step(t))
+
+    def turn_values():
+        swap_wait(1)
+        lax.fori_loop(0, 6, turn, 0)
+
+    def make_marks():
+        arrive(gather(3, 3))
+        lax.fori_loop(0, 16, expand, 0)
+
+    def ready_audio():
+        swap_wait(0)
+        swap_marks().wait_recv()
+        arrive(gather(0, 3))
+
+    def turn_window_all():
+        arrive(gather(2, 3))
+
+    def ready_video():
+        swap_wait(2)
+        arrive(gather(1, 3))
+
+    def finish_half(half):
+        reduce_end(half)
+        start(results(half))
+
+    steps = {
+        "xKs": lambda: x_next(1), "xVs": lambda: x_next(2), "vqs": lambda: swap_start(2),
+        "vt": turn_values, "ex": make_marks, "tw": turn_window_all,
+        "w0": lambda: start(video_copies(0)), "w1": lambda: start(video_copies(1)), "w2": lambda: start(video_copies(2)),
+    }
+    for t, name in enumerate("QKV"):
+        for stage in range(4):
+            steps[f"{stage + 1}{name}"] = lambda t=t, stage=stage: take(t, stage)
+    for half in range(2):
+        steps[f"p{half}"] = lambda half=half: place_all(half)
+        steps[f"r1_{half}"] = lambda half=half: reduce_start(half)
+        steps[f"r2_{half}"] = lambda half=half: reduce_pass(half)
+        steps[f"ca_{half}"] = lambda half=half: reduce_cross(half)
+        steps[f"cb_{half}"] = lambda half=half: reduce_cross_pass(half)
+        steps[f"o_{half}"] = lambda half=half: finish_half(half)
+
+    parts = {"": [], "A": [], "B": [], "X": [], "T": [], "Y": []}
+    part_now, at = "", None
+    for name in ORDER:
+        if isinstance(name, int):
+            at = name
+        elif name in parts:
+            part_now, at = name, None
+        else:
+            parts[part_now].append((at, steps[name]))
+
+    def run(name):
+        for _, step in parts[name]:
+            step()
+
+    run("")
+    ready_audio()
+    pipeline(30, 4, audio_scores, audio_finish, parts["A"])
+    run("B")
+    ready_video()
+    video_weights(parts["X"])
+    run("T")
+    video_values(parts["Y"])
 
     for t in range(4):
         sent(x_step(t))
@@ -580,9 +603,11 @@
             pltpu.VMEM((2, 4, 4, 64, HD), BF),
             pltpu.VMEM((32, HD), BF),
             pltpu.VMEM((6, HD + 16, 1024), BF),
-            pltpu.VMEM((6, HD + 16, BLOCKS * HD), BF),
-            pltpu.VMEM((BLOCKS * HD, 256), F32),
-            pltpu.VMEM((BLOCKS * HD, 256), F32),
+            pltpu.VMEM((1024, 256), F32),
+            pltpu.VMEM((1024, 256), F32),
+            pltpu.VMEM((512, BLOCKS * HD), F32),
+            pltpu.VMEM((512, BLOCKS * HD), F32),
+            pltpu.VMEM((12, 512, BLOCKS * HD), BF),
             pltpu.VMEM((6, BLOCKS, 8, HD), F32),
             pltpu.VMEM((6, BLOCKS, 8, HD), F32),
             pltpu.VMEM((2, BLOCKS, STAT, HD), BF),

time: 110 us -> 107 us (0.973)
  Pallas kernels: 105 us -> 103 us
    pallas_call x1, Pallas kernels: 105 us -> 103 us  [on_device(): pl.pallas_call(kernel, out_shape=(jax.ShapeDtypeStruct(video_q.shape, BF)...]
where the time goes in v4:
time: 107 us
  Pallas kernels  103 us (96%)
  local copies, waits for them, and re-layouts  3.37 us (3%)
    pallas_call x1, Pallas kernels, on_device(): pl.pallas_call(kernel, out_shape=(jax.ShapeDtypeStruct(video_q.shape, BF)...  103 us
    unnamed x4, local copies, waits for them, and re-layouts  3.37 us

profile of v4, /device:TPU:1, one launch (start us, length us, event | category | flops | bytes accessed | tf_op | source)
XLA Modules:
  0.0 107.3 jit_solution(15636395571959921568)
XLA Ops:
  0.6 103.3 %shard_map.95 = (bf16[512,1536]{1,0:T(8,128)(2,1)}, bf16[64,1536]{1,0:T(8,128)(2,1)}) custom-call(s32[512]{0:T(512)} %clip_smem.1, s32[4,128]{1,0:T(4,128)} %bitcast.2, s32[1,64]{1,0:T(1,128)} %bitcast.3, bf16[512,1536]{1,0:T(8,128)(2,1)} %vq_hbm.1, bf16[512,1536]{1,0:T(8,128)(2,1)} %vk_hbm.1, bf16[512,1536]{1,0:T(8,128)(2,1)} %vv_hbm.1, ...), custom_call_target="tpu_custom_call" | custom-call | tf_op jit(solution)/shard_map/pallas_call | solution.py:581
  103.9 0.0 copy-start
  103.9 2.7 %copy.12 = bf16[512,1536]{1,0:T(8,128)(2,1)} copy(bf16[512,1536]{1,0:T(8,128)(2,1)} %get-tuple-element.4) | data formatting | bytes 3145728
  106.6 0.0 copy-done
  106.6 0.7 copy.13
Async XLA Ops:
  103.9 2.7 %copy-start = (bf16[64,1536]{1,0:T(8,128)(2,1)S(1)}, bf16[64,1536]{1,0:T(8,128)(2,1)}, u32[]{:S(2)}) copy-start(bf16[64,1536]{1,0:T(8,128)(2,1)} %get-tuple-element.5) | copy-start | bytes 589828

commit v5 on v4

--- a/solution.py
+++ b/solution.py
@@ -21,12 +21,9 @@
 
 
 ORDER = (
-    "1Q", "2Q", "3Q", "vqs", "xKs", "xVs", "1K", "1V", "4Q", "ex", "2K", "vt", "2V", "3K",
-    "A", 2, "3V", 8, "4K", 12, "p0", 13, "r1_0",
-    "B", "p1", "r1_1",
-    "X", 3, "4V", 5, "r2_0", "r2_1",
-    "T", "tw", "ca_0", "ca_1",
-    "Y", 1, "cb_0", "cb_1", "w0", 2, "o_0", 3, "o_1", "w1", 5, "w2",
+    "1Q", "xKs", "2Q", "xVs", "1K", "3Q", "1V", "vt", "2K", "4Q", "2V", "ex", "3K", "vqs", "A", 1, "3V", 7,
+    "p0", "4K", 11, "r1_0", "B", "p1", "r1_1", "X", 1, "4V", 3, "r2_0", "r2_1", 5, "ca_0", "T", "ca_1", "tw",
+    "Y", 0, "cb_0", 1, "cb_1", 3, "o_0", 4, "w1", "o_1", "w0", 5, "w2",
 )
 
 

time: 107 us -> 103 us (0.963)
  Pallas kernels: 103 us -> 98.8 us
    pallas_call x1, Pallas kernels: 103 us -> 98.8 us  [on_device(): pl.pallas_call(kernel, out_shape=(jax.ShapeDtypeStruct(video_q.shape, BF)...]
where the time goes in v5:
time: 103 us
  Pallas kernels  98.8 us (96%)
  local copies, waits for them, and re-layouts  3.37 us (3%)
    pallas_call x1, Pallas kernels, on_device(): pl.pallas_call(kernel, out_shape=(jax.ShapeDtypeStruct(video_q.shape, BF)...  98.8 us
    unnamed x4, local copies, waits for them, and re-layouts  3.37 us

profile of v5, /device:TPU:1, one launch (start us, length us, event | category | flops | bytes accessed | tf_op | source)
XLA Modules:
  0.0 102.8 jit_solution(16829449627713483181)
XLA Ops:
  0.6 98.8 %shard_map.95 = (bf16[512,1536]{1,0:T(8,128)(2,1)}, bf16[64,1536]{1,0:T(8,128)(2,1)}) custom-call(s32[512]{0:T(512)} %clip_smem.1, s32[4,128]{1,0:T(4,128)} %bitcast.2, s32[1,64]{1,0:T(1,128)} %bitcast.3, bf16[512,1536]{1,0:T(8,128)(2,1)} %vq_hbm.1, bf16[512,1536]{1,0:T(8,128)(2,1)} %vk_hbm.1, bf16[512,1536]{1,0:T(8,128)(2,1)} %vv_hbm.1, ...), custom_call_target="tpu_custom_call" | custom-call | tf_op jit(solution)/shard_map/pallas_call | solution.py:578
  99.4 0.0 copy-start
  99.4 2.7 %copy.12 = bf16[512,1536]{1,0:T(8,128)(2,1)} copy(bf16[512,1536]{1,0:T(8,128)(2,1)} %get-tuple-element.4) | data formatting | bytes 3145728
  102.1 0.0 copy-done
  102.1 0.7 copy.13
Async XLA Ops:
  99.4 2.7 %copy-start = (bf16[64,1536]{1,0:T(8,128)(2,1)S(1)}, bf16[64,1536]{1,0:T(8,128)(2,1)}, u32[]{:S(2)}) copy-start(bf16[64,1536]{1,0:T(8,128)(2,1)} %get-tuple-element.5) | copy-start | bytes 589828

commit v6 on v5

--- a/solution.py
+++ b/solution.py
@@ -21,8 +21,11 @@
 
 
 ORDER = (
-    "1Q", "xKs", "2Q", "xVs", "1K", "3Q", "1V", "vt", "2K", "4Q", "2V", "ex", "3K", "vqs", "A", 1, "3V", 7,
-    "p0", "4K", 11, "r1_0", "B", "p1", "r1_1", "X", 1, "4V", 3, "r2_0", "r2_1", 5, "ca_0", "T", "ca_1", "tw",
+    "1Q", "xKs", "2Q", "xVs", "1K", "3Q", "1V", "vt", "2K", "4Q", "2V", "ex", "3K", "vqs",
+    "A", 0, "3V", 5, "p0", "4K", 8, "r1_0",
+    "B", "p1", "r1_1",
+    "X", 1, "4V", 3, "r2_0", "r2_1", 5, "ca_0",
+    "T", "ca_1", "tw",
     "Y", 0, "cb_0", 1, "cb_1", 3, "o_0", 4, "w1", "o_1", "w0", 5, "w2",
 )
 
@@ -30,7 +33,7 @@
 def kernel(
     clip_smem, video_clip, audio_clip, vq_hbm, vk_hbm, vv_hbm, aq_hbm, ak_hbm, av_hbm,
     vout_hbm, aout_hbm,
-    vq, vk, vv, ve, aq, ak, av, mk, am, mk_own, vt, buf_c, buf_d, buf_a, buf_b, wb, tops, sums, window, part, got1, got2, vo, ao,
+    vq, vk, vv, ve, aq, ak, av, mk, am, mk_own, buf_c, buf_d, wt_c, wt_d, high_c, high_d, buf_a, buf_b, wb, tops, sums, window, part, got1, got2, vo, ao,
     x_send, x_recv, g_send, g_recv, v_send, v_recv, v_local, r_send, r_recv, o_send, o_recv, w_send, w_recv, w_local,
 ):
     g = lax.axis_index("grp")
@@ -186,12 +189,6 @@
         ve[pl.ds(at, HD), :] = jnp.where(same, 0.0, FAR).T.astype(BF)
     swap_marks().start()
 
-    def turn(h, carry):
-        cols = pl.ds(pl.multiple_of(h * HD, HD), HD)
-        vt[h, pl.ds(0, HD), :] = vv[:, cols].T
-        vt[h, pl.ds(HD, 16), :] = jnp.ones((16, 1024), BF)
-        return carry
-
     lanes = clips.astype(F32)
 
     def expand(i, carry):
@@ -226,65 +223,70 @@
                     if where == at:
                         event()
 
-    def pipeline(units, sizes, scores_of, finish, events):
-        def both(u_scores, u_out, buf_scores, buf_out, top):
-            q, k_of = scores_of(u_scores)
-            store = None
-            if u_out is not None:
-                top = jnp.max(top, axis=0, keepdims=True) * SCALE
-                top, use, store = finish(u_out, top)
-            high, total = None, None
-            for c in range(sizes):
+    lane = lax.broadcasted_iota(jnp.int32, (HD, HD), 1)
+
+    def audio_step(unit_scores, unit_weights, unit_values):
+        if unit_scores is not None:
+            u, buf = unit_scores
+            cols = pl.ds(pl.multiple_of(u // 2 * HD, HD), HD)
+            blocks = [5 * lax.rem(u, 2) + i for i in range(5)]
+            q = jnp.concatenate([piece for i in blocks for piece in pieces(aq, i, cols)], axis=0)
+            mark = jnp.concatenate([piece for i in blocks for piece in pieces(am, i, marks)], axis=0)
+            q = jnp.concatenate([q, mark], axis=1)
+        if unit_values is not None:
+            h, tile, weights, high = unit_values[0] // 2, lax.rem(unit_values[0], 2), unit_values[1], unit_values[2]
+            v = jnp.concatenate([vv[:, pl.ds(pl.multiple_of(h * HD, HD), HD)], jnp.ones((1024, HD), BF)], axis=1)
+            out = jnp.dot(weights[...], v, preferred_element_type=F32)
+        row = 0
+        for c in range(4):
+            if unit_scores is not None:
                 rows = pl.ds(c * 256, 256)
-                scores = lax.dot_general(k_of(c), q, (((1,), (1,)), ((), ())), preferred_element_type=F32)
-                buf_scores[rows, :] = scores
-                best = jnp.max(scores.reshape(32, 8, 256), axis=0)
-                high = best if high is None else jnp.maximum(high, best)
-                if u_out is not None:
-                    weights = jnp.exp2(buf_out[rows, :] * SCALE - top).astype(BF)
-                    out = use(c, weights)
-                    if store is not None:
-                        total = out if total is None else total + out
-            if store is not None:
-                store(total, top)
-            return high
-
-        def body(i, top):
+                k = jnp.concatenate([vk[rows, cols], ve[rows, :]], axis=1)
+                buf[:, c * 256 : (c + 1) * 256] = lax.dot_general(
+                    q, k, (((1,), (1,)), ((), ())), preferred_element_type=F32
+                )
+            if unit_weights is not None:
+                scores_w, weights_w, high_w = unit_weights
+                for _ in range(10):
+                    scores = scores_w[row : row + 16, :]
+                    top = jnp.maximum(jnp.max(scores, axis=1, keepdims=True) * SCALE, LOW).astype(BF).astype(F32)
+                    weights_w[row : row + 16, :] = jnp.exp2(scores * SCALE - top).astype(BF)
+                    high_w[row : row + 16, :] = jnp.broadcast_to(top, (16, HD))
+                    row += 16
+        if unit_values is not None:
+            where = pl.ds(pl.multiple_of(lax.rem(h, 3) * HD, HD), HD)
+            for b in range(5):
+                rows = slice(b * HD, (b + 1) * HD)
+                window[h // 3, 5 * tile + b, where, :] = out[rows, :HD].T.astype(BF)
+                stats = jnp.where(lane < 8, high[rows, :], out[rows, HD:]).T
+                tops[h, 5 * tile + b] = stats[0:8]
+                sums[h, 5 * tile + b] = stats[8:16]
+
+    def audio(events):
+        even, odd = (buf_c, wt_c, high_c), (buf_d, wt_d, high_d)
+
+        def body(i, carry):
             u = 2 * i
-            top = both(u + 1, u, buf_d, buf_c, top)
-            top = both(jnp.minimum(u + 2, units - 1), u + 1, buf_c, buf_d, top)
-            run_events(i, events)
-            return top
-
-        lax.fori_loop(0, units // 2, body, both(0, None, buf_c, None, None))
-
-    def audio_scores(u):
-        h, tile = u // 5, lax.rem(u, 5)
-        cols = pl.ds(pl.multiple_of(h * HD, HD), HD)
-        mark = jnp.concatenate(pieces(am, 2 * tile, marks) + pieces(am, 2 * tile + 1, marks), axis=0)
-        q = jnp.concatenate(pieces(aq, 2 * tile, cols) + pieces(aq, 2 * tile + 1, cols), axis=0)
-
-        def k_of(c):
-            rows = pl.ds(c * 256, 256)
-            return jnp.concatenate([vk[rows, cols], ve[rows, :]], axis=1)
-
-        return jnp.concatenate([q, mark], axis=1), k_of
-
-    def audio_finish(u, top):
-        h, tile = u // 5, lax.rem(u, 5)
-        top = jnp.maximum(top, LOW).astype(BF).astype(F32)
-
-        def use(c, weights):
-            return jnp.dot(vt[h, :, pl.ds(c * 256, 256)], weights, preferred_element_type=F32)
-
-        def store(out, top):
-            where = pl.ds(pl.multiple_of(lax.rem(h, 3) * HD, HD), HD)
-            for b in range(2):
-                window[h // 3, 2 * tile + b, where, :] = out[:HD, b * HD : (b + 1) * HD].astype(BF)
-                tops[h, 2 * tile + b] = jnp.broadcast_to(top[:, b * HD : (b + 1) * HD], (8, HD))
-                sums[h, 2 * tile + b] = jnp.broadcast_to(out[HD : HD + 1, b * HD : (b + 1) * HD], (8, HD))
-
-        return top, use, store
+            audio_step((u + 2, buf_c), odd, (u, wt_c, high_c))
+            run_events(u, events)
+            audio_step((u + 3, buf_d), even, (u + 1, wt_d, high_d))
+            run_events(u + 1, events)
+            return carry
+
+        audio_step((0, buf_c), None, None)
+        audio_step((1, buf_d), even, None)
+        lax.fori_loop(0, 5, body, 0)
+        audio_step(None, odd, (10, wt_c, high_c))
+        audio_step(None, None, (11, wt_d, high_d))
+
+    def run_events(i, events):
+        for at in sorted({at for at, _ in events}):
+
+            @pl.when(i == at)
+            def _():
+                for where, event in events:
+                    if where == at:
+                        event()
 
     empty = jnp.where(lax.broadcasted_iota(jnp.int32, (16, HD), 0) < 3, LOW, 0.0)
 
@@ -488,7 +490,6 @@
 
     def turn_values():
         swap_wait(1)
-        lax.fori_loop(0, 6, turn, 0)
 
     def make_marks():
         arrive(gather(3, 3))
@@ -542,7 +543,7 @@
 
     run("")
     ready_audio()
-    pipeline(30, 4, audio_scores, audio_finish, parts["A"])
+    audio(parts["A"])
     run("B")
     ready_video()
     video_weights(parts["X"])
@@ -599,9 +600,12 @@
             pltpu.VMEM((2, 4, 4, 32, HD), BF),
             pltpu.VMEM((2, 4, 4, 64, HD), BF),
             pltpu.VMEM((32, HD), BF),
-            pltpu.VMEM((6, HD + 16, 1024), BF),
-            pltpu.VMEM((1024, 256), F32),
-            pltpu.VMEM((1024, 256), F32),
+            pltpu.VMEM((640, 1024), F32),
+            pltpu.VMEM((640, 1024), F32),
+            pltpu.VMEM((640, 1024), BF),
+            pltpu.VMEM((640, 1024), BF),
+            pltpu.VMEM((640, HD), F32),
+            pltpu.VMEM((640, HD), F32),
             pltpu.VMEM((512, BLOCKS * HD), F32),
             pltpu.VMEM((512, BLOCKS * HD), F32),
             pltpu.VMEM((12, 512, BLOCKS * HD), BF),
@@ -629,7 +633,7 @@
             dma((3,)),
         ],
         compiler_params=pltpu.CompilerParams(
-            collective_id=0, has_side_effects=True, vmem_limit_bytes=56 * 1024 * 1024
+            collective_id=0, has_side_effects=True, vmem_limit_bytes=60 * 1024 * 1024
         ),
     )(
         video_clip, video_clip.reshape(4, HD), audio_clip.reshape(1, 64), video_q, video_k, video_v, audio_q, audio_k,

time: 103 us -> 103 us (level)
  no operation moved by 1% of the time
where the time goes in v6:
time: 103 us
  Pallas kernels  98.8 us (96%)
  local copies, waits for them, and re-layouts  3.37 us (3%)
    pallas_call x1, Pallas kernels, on_device(): pl.pallas_call(kernel, out_shape=(jax.ShapeDtypeStruct(video_q.shape, BF)...  98.8 us
    unnamed x4, local copies, waits for them, and re-layouts  3.37 us

profile of v6, /device:TPU:1, one launch (start us, length us, event | category | flops | bytes accessed | tf_op | source)
XLA Modules:
  0.0 102.8 jit_solution(3104431419063039362)
XLA Ops:
  0.6 98.8 %shard_map.95 = (bf16[512,1536]{1,0:T(8,128)(2,1)}, bf16[64,1536]{1,0:T(8,128)(2,1)}) custom-call(s32[512]{0:T(512)} %clip_smem.1, s32[4,128]{1,0:T(4,128)} %bitcast.2, s32[1,64]{1,0:T(1,128)} %bitcast.3, bf16[512,1536]{1,0:T(8,128)(2,1)} %vq_hbm.1, bf16[512,1536]{1,0:T(8,128)(2,1)} %vk_hbm.1, bf16[512,1536]{1,0:T(8,128)(2,1)} %vv_hbm.1, ...), custom_call_target="tpu_custom_call" | custom-call | tf_op jit(solution)/shard_map/pallas_call | solution.py:579
  99.4 0.0 copy-start
  99.4 2.7 %copy.12 = bf16[512,1536]{1,0:T(8,128)(2,1)} copy(bf16[512,1536]{1,0:T(8,128)(2,1)} %get-tuple-element.4) | data formatting | bytes 3145728
  102.1 0.0 copy-done
  102.1 0.7 copy.13
Async XLA Ops:
  99.4 2.7 %copy-start = (bf16[64,1536]{1,0:T(8,128)(2,1)S(1)}, bf16[64,1536]{1,0:T(8,128)(2,1)}, u32[]{:S(2)}) copy-start(bf16[64,1536]{1,0:T(8,128)(2,1)} %get-tuple-element.5) | copy-start | bytes 589828

commit v7 on v6

--- a/solution.py
+++ b/solution.py
@@ -1,3 +1,4 @@
+import functools
 import math
 
 import jax
@@ -21,19 +22,18 @@
 
 
 ORDER = (
-    "1Q", "xKs", "2Q", "xVs", "1K", "3Q", "1V", "vt", "2K", "4Q", "2V", "ex", "3K", "vqs",
-    "A", 0, "3V", 5, "p0", "4K", 8, "r1_0",
-    "B", "p1", "r1_1",
-    "X", 1, "4V", 3, "r2_0", "r2_1", 5, "ca_0",
-    "T", "ca_1", "tw",
-    "Y", 0, "cb_0", 1, "cb_1", 3, "o_0", 4, "w1", "o_1", "w0", 5, "w2",
+    "1Q0", "sQ1", "2Q0", "sK0", "1Q1", "3Q0", "2Q1", "sK1", "1K0", "3Q1", "4Q0", "sV0", "1K1", "1V0", "2K0",
+    "sV1", "4Q1", "ex", "A", -2, "2K1", -1, "1V1", "2V0", "3K0", "vqs", 2, "2V1", "3K1", "rQ1", 3, "3V0", 5,
+    "4K0", 6, "p0", 8, "4K1", "r1_0", "B", "p1", "r1_1", "X", -1, "rK1", 3, "3V1", "r2_0", "4V0", 6, "r2_1",
+    10, "ca_0", "4V1", "tw0", "T", "ca_1", "Y", 1, "cb_0", 2, "w0", "cb_1", "tw1", 3, "o_0", "w1", 4, "o_1",
+    5, "w2",
 )
 
 
 def kernel(
     clip_smem, video_clip, audio_clip, vq_hbm, vk_hbm, vv_hbm, aq_hbm, ak_hbm, av_hbm,
     vout_hbm, aout_hbm,
-    vq, vk, vv, ve, aq, ak, av, mk, am, mk_own, buf_c, buf_d, wt_c, wt_d, high_c, high_d, buf_a, buf_b, wb, tops, sums, window, part, got1, got2, vo, ao,
+    vq, vk, vv, ve, aq0, aq1, ak0, ak1, av0, av1, mk, am, mk_own, buf_c, buf_d, wt_c, wt_d, high_c, high_d, buf_a, buf_b, wb, tops, sums, window, part, got1, got2, vo, ao,
     x_send, x_recv, g_send, g_recv, v_send, v_recv, v_local, r_send, r_recv, o_send, o_recv, w_send, w_recv, w_local,
 ):
     g = lax.axis_index("grp")
@@ -83,13 +83,15 @@
     def columns(half, width):
         return pl.ds(pl.multiple_of(half * width, 128), width)
 
-    tensors = ((aq_hbm, aq), (ak_hbm, ak), (av_hbm, av), (mk_own, mk))
+    aq, ak, av = (aq0, aq1), (ak0, ak1), (av0, av1)
+    tensors = [(src, dst[half], half) for src, dst in ((aq_hbm, aq), (ak_hbm, ak), (av_hbm, av)) for half in (0, 1)]
+    tensors.append((mk_own, mk, None))
 
     def x_copies(t, sender):
-        src, dst = tensors[t]
+        src, dst, half = tensors[t]
         return [
             remote(
-                src if t == 3 else src.at[:, pl.ds(cc * 768, 768)], dst.at[sender, z, y], x_send.at[t, cc],
+                src if half is None else src.at[:, pl.ds(cc * 768 + half * 384, 384)], dst.at[sender, z, y], x_send.at[t, cc],
                 x_recv.at[t, sender], device(gm, z, y, cc),
             )
             for cc in (0, 1)
@@ -109,7 +111,7 @@
 
     def gather(t, stage):
         x = tensors[t][1]
-        rows = x.shape[3] // 2
+        rows = 16 if t == 6 else 32
         low, high = pl.ds(0, rows), pl.ds(rows, rows)
         first, last = pl.ds(0, 2), pl.ds(2, 2)
         plan = (
@@ -181,7 +183,7 @@
     numbers = (audio_clip[...] - gm * CLIPS).astype(F32)
     numbers = jnp.concatenate([numbers, numbers], axis=1)
     mk_own[...] = jnp.broadcast_to(numbers, (32, HD)).astype(BF)
-    start(x_step(3))
+    start(x_step(6))
     clips = lax.broadcasted_iota(jnp.int32, (HD, HD), 0)
     for i in range(4):
         same = video_clip[i : i + 1, :] - g * CLIPS == clips
@@ -203,35 +205,28 @@
     def block(i):
         return jnp.bitwise_and(first + i, 15)
 
-    def pieces(ref, i, cols):
+    def pieces(ref, i, h):
         b, a = block(i - 1), block(i)
-        return [ref[1, b // 4, jnp.bitwise_and(b, 3), :, cols], ref[0, a // 4, jnp.bitwise_and(a, 3), :, cols]]
-
-    marks = pl.ds(0, HD)
+        where = (1, b // 4, jnp.bitwise_and(b, 3)), (0, a // 4, jnp.bitwise_and(a, 3))
+        if h is None:
+            return [ref[at] for at in where]
+        cols = pl.ds(pl.multiple_of(lax.rem(h, 3) * HD, HD), HD)
+        return [ref[(*at, slice(None), cols)] for at in where]
 
     def packed(top, total):
         high = total.astype(BF).astype(F32)
         gap = jnp.zeros((1, HD), F32)
         return jnp.concatenate([top, gap, total - high, gap, high, jnp.zeros((5, HD), F32)], axis=0)
 
-    def run_events(i, events):
-        for at in sorted({at for at, _ in events}):
-
-            @pl.when(i == at)
-            def _():
-                for where, event in events:
-                    if where == at:
-                        event()
-
     lane = lax.broadcasted_iota(jnp.int32, (HD, HD), 1)
 
     def audio_step(unit_scores, unit_weights, unit_values):
         if unit_scores is not None:
-            u, buf = unit_scores
+            u, buf, ref = unit_scores
             cols = pl.ds(pl.multiple_of(u // 2 * HD, HD), HD)
             blocks = [5 * lax.rem(u, 2) + i for i in range(5)]
-            q = jnp.concatenate([piece for i in blocks for piece in pieces(aq, i, cols)], axis=0)
-            mark = jnp.concatenate([piece for i in blocks for piece in pieces(am, i, marks)], axis=0)
+            q = jnp.concatenate([piece for i in blocks for piece in pieces(ref, i, u // 2)], axis=0)
+            mark = jnp.concatenate([piece for i in blocks for piece in pieces(am, i, None)], axis=0)
             q = jnp.concatenate([q, mark], axis=1)
         if unit_values is not None:
             h, tile, weights, high = unit_values[0] // 2, lax.rem(unit_values[0], 2), unit_values[1], unit_values[2]
@@ -265,28 +260,34 @@
     def audio(events):
         even, odd = (buf_c, wt_c, high_c), (buf_d, wt_d, high_d)
 
-        def body(i, carry):
+        def body(ref, lo, hi, i, carry):
             u = 2 * i
-            audio_step((u + 2, buf_c), odd, (u, wt_c, high_c))
-            run_events(u, events)
-            audio_step((u + 3, buf_d), even, (u + 1, wt_d, high_d))
-            run_events(u + 1, events)
+            audio_step((u + 2, buf_c, ref), odd, (u, wt_c, high_c))
+            run_events(u, events, range(lo, hi, 2))
+            audio_step((u + 3, buf_d, ref), even, (u + 1, wt_d, high_d))
+            run_events(u + 1, events, range(lo + 1, hi, 2))
             return carry
 
-        audio_step((0, buf_c), None, None)
-        audio_step((1, buf_d), even, None)
-        lax.fori_loop(0, 5, body, 0)
+        audio_step((0, buf_c, aq[0]), None, None)
+        run_now(-2, events)
+        audio_step((1, buf_d, aq[0]), even, None)
+        run_now(-1, events)
+        lax.fori_loop(0, 2, functools.partial(body, aq[0], 0, 4), 0)
+        lax.fori_loop(2, 5, functools.partial(body, aq[1], 4, 10), 0)
         audio_step(None, odd, (10, wt_c, high_c))
         audio_step(None, None, (11, wt_d, high_d))
 
-    def run_events(i, events):
-        for at in sorted({at for at, _ in events}):
+    def run_now(at, events):
+        for where, event in events:
+            if where == at:
+                event()
+
+    def run_events(i, events, steps_here):
+        for at in sorted({at for at, _ in events if at in steps_here}):
 
             @pl.when(i == at)
             def _():
-                for where, event in events:
-                    if where == at:
-                        event()
+                run_now(at, events)
 
     empty = jnp.where(lax.broadcasted_iota(jnp.int32, (16, HD), 0) < 3, LOW, 0.0)
 
@@ -421,19 +422,19 @@
             for i, (rows, dev) in enumerate(((pl.ds(64, 64), result_low), (pl.ds(0, 64), result_high)))
         ]
 
-    def rows_of(ref, i, cols):
-        return jnp.concatenate(pieces(ref, 2 * i, cols) + pieces(ref, 2 * i + 1, cols), axis=0)
+    def rows_of(ref, i, h):
+        return jnp.concatenate(pieces(ref, 2 * i, h) + pieces(ref, 2 * i + 1, h), axis=0)
 
     def video_unit(u):
         cols = pl.ds(pl.multiple_of(u // 2 * HD, HD), HD)
         return cols, pl.ds(pl.multiple_of(lax.rem(u, 2) * 512, 512), 512)
 
-    def video_both(u_scores, u_out, buf_scores, buf_out):
+    def video_both(u_scores, ref, u_out, buf_scores, buf_out):
         cols, here = video_unit(u_scores)
         q = jnp.concatenate([vq[here, cols], ve[here, :]], axis=1)
         row = 0
         for c in range(5):
-            k = jnp.concatenate([rows_of(ak, c, cols), rows_of(am, c, marks)], axis=1)
+            k = jnp.concatenate([rows_of(ref, c, u_scores // 2), rows_of(am, c, None)], axis=1)
             buf_scores[:, c * 256 : (c + 1) * 256] = lax.dot_general(
                 q, k, (((1,), (1,)), ((), ())), preferred_element_type=F32
             )
@@ -445,28 +446,33 @@
                     row += 16
 
     def video_weights(events):
-        def body(i, carry):
+        def body(refs, lo, hi, i, carry):
             u = 2 * i
-            video_both(u + 1, u, buf_b, buf_a)
-            video_both(jnp.minimum(u + 2, 11), u + 1, buf_a, buf_b)
-            run_events(i, events)
+            video_both(u + 1, refs[0], u, buf_b, buf_a)
+            run_events(u, events, range(lo, hi, 2))
+            video_both(jnp.minimum(u + 2, 11), refs[1], u + 1, buf_a, buf_b)
+            run_events(u + 1, events, range(lo + 1, hi, 2))
             return carry
 
-        video_both(0, None, buf_a, None)
-        lax.fori_loop(0, 6, body, 0)
+        video_both(0, ak[0], None, buf_a, None)
+        run_now(-1, events)
+        lax.fori_loop(0, 2, functools.partial(body, (ak[0], ak[0]), 0, 4), 0)
+        lax.fori_loop(2, 3, functools.partial(body, (ak[0], ak[1]), 4, 6), 0)
+        lax.fori_loop(3, 6, functools.partial(body, (ak[1], ak[1]), 6, 12), 0)
 
     def video_values(events):
-        def body(i, carry):
+        def body(ref, lo, hi, i, carry):
             cols, _ = video_unit(2 * i)
-            v = jnp.concatenate([rows_of(av, c, cols) for c in range(5)], axis=0)
+            v = jnp.concatenate([rows_of(ref, c, i) for c in range(5)], axis=0)
             v = jnp.concatenate([v, jnp.ones((BLOCKS * HD, HD), BF)], axis=1)
             for j in range(2):
                 out = jnp.dot(wb[2 * i + j], v, preferred_element_type=F32)
                 vo[pl.ds(j * 512, 512), cols] = (out[:, :HD] / out[:, HD:]).astype(BF)
-            run_events(i, events)
+            run_events(i, events, range(lo, hi))
             return carry
 
-        lax.fori_loop(0, 6, body, 0)
+        lax.fori_loop(0, 3, functools.partial(body, av[0], 0, 3), 0)
+        lax.fori_loop(3, 6, functools.partial(body, av[1], 3, 6), 0)
 
     def video_copies(i):
         cols = pl.ds(i * 256, 256)
@@ -477,7 +483,7 @@
         )
 
     def take(t, stage):
-        for tensor in (3, 0) if t == 0 else (t,):
+        for tensor in (6, 0) if t == 0 else (t,):
             if stage == 0:
                 x_wait(tensor)
             else:
@@ -488,35 +494,31 @@
         x_wait(t - 1)
         start(x_step(t))
 
-    def turn_values():
-        swap_wait(1)
-
     def make_marks():
-        arrive(gather(3, 3))
+        arrive(gather(6, 3))
         lax.fori_loop(0, 16, expand, 0)
 
     def ready_audio():
         swap_wait(0)
+        swap_wait(1)
         swap_marks().wait_recv()
         arrive(gather(0, 3))
 
-    def turn_window_all():
-        arrive(gather(2, 3))
-
     def ready_video():
         swap_wait(2)
-        arrive(gather(1, 3))
+        arrive(gather(2, 3))
 
     def finish_half(half):
         reduce_end(half)
         start(results(half))
 
     steps = {
-        "xKs": lambda: x_next(1), "xVs": lambda: x_next(2), "vqs": lambda: swap_start(2),
-        "vt": turn_values, "ex": make_marks, "tw": turn_window_all,
+        "vqs": lambda: swap_start(2), "ex": make_marks, "rQ1": lambda: arrive(gather(1, 3)), "rK1": lambda: arrive(gather(3, 3)),
+        "tw0": lambda: arrive(gather(4, 3)), "tw1": lambda: arrive(gather(5, 3)),
         "w0": lambda: start(video_copies(0)), "w1": lambda: start(video_copies(1)), "w2": lambda: start(video_copies(2)),
     }
-    for t, name in enumerate("QKV"):
+    for t, name in enumerate(("Q0", "Q1", "K0", "K1", "V0", "V1")):
+        steps[f"s{name}"] = lambda t=t: x_next(t)
         for stage in range(4):
             steps[f"{stage + 1}{name}"] = lambda t=t, stage=stage: take(t, stage)
     for half in range(2):
@@ -550,7 +552,7 @@
     run("T")
     video_values(parts["Y"])
 
-    for t in range(4):
+    for t in range(7):
         sent(x_step(t))
         for stage in range(4):
             sent(gather(t, stage))
@@ -594,9 +596,12 @@
             pltpu.VMEM((1024, 768), BF),
             pltpu.VMEM((1024, 768), BF),
             pltpu.VMEM((1024, HD), BF),
-            pltpu.VMEM((2, 4, 4, 64, 768), BF),
-            pltpu.VMEM((2, 4, 4, 64, 768), BF),
-            pltpu.VMEM((2, 4, 4, 64, 768), BF),
+            pltpu.VMEM((2, 4, 4, 64, 384), BF),
+            pltpu.VMEM((2, 4, 4, 64, 384), BF),
+            pltpu.VMEM((2, 4, 4, 64, 384), BF),
+            pltpu.VMEM((2, 4, 4, 64, 384), BF),
+            pltpu.VMEM((2, 4, 4, 64, 384), BF),
+            pltpu.VMEM((2, 4, 4, 64, 384), BF),
             pltpu.VMEM((2, 4, 4, 32, HD), BF),
             pltpu.VMEM((2, 4, 4, 64, HD), BF),
             pltpu.VMEM((32, HD), BF),
@@ -617,10 +622,10 @@
             pltpu.VMEM((2, 3, ROWS, HD), BF),
             pltpu.VMEM((1024, 768), BF),
             pltpu.VMEM((HD, 768), BF),
-            dma((4, 2)),
-            dma((4, 2)),
-            dma((4, 16)),
-            dma((4, 16)),
+            dma((7, 2)),
+            dma((7, 2)),
+            dma((7, 16)),
+            dma((7, 16)),
             dma((4,)),
             dma((4,)),
             dma((3,)),

time: 103 us -> 100 us (0.971)
  Pallas kernels: 98.8 us -> 95.9 us
    pallas_call x1, Pallas kernels: 98.8 us -> 95.9 us  [on_device(): pl.pallas_call(kernel, out_shape=(jax.ShapeDtypeStruct(video_q.shape, BF)...]
where the time goes in v7:
time: 100 us; the launch traced here: 99.9 us
  Pallas kernels  95.9 us (96%)
  local copies, waits for them, and re-layouts  3.37 us (3%)
    pallas_call x1, Pallas kernels, on_device(): pl.pallas_call(kernel, out_shape=(jax.ShapeDtypeStruct(video_q.shape, BF)...  95.9 us
    unnamed x4, local copies, waits for them, and re-layouts  3.37 us

profile of v7, /device:TPU:1, one launch (start us, length us, event | category | flops | bytes accessed | tf_op | source)
XLA Modules:
  0.0 99.9 jit_solution(15847235155224230834)
XLA Ops:
  0.6 95.9 %shard_map.95 = (bf16[512,1536]{1,0:T(8,128)(2,1)}, bf16[64,1536]{1,0:T(8,128)(2,1)}) custom-call(s32[512]{0:T(512)} %clip_smem.1, s32[4,128]{1,0:T(4,128)} %bitcast.2, s32[1,64]{1,0:T(1,128)} %bitcast.3, bf16[512,1536]{1,0:T(8,128)(2,1)} %vq_hbm.1, bf16[512,1536]{1,0:T(8,128)(2,1)} %vk_hbm.1, bf16[512,1536]{1,0:T(8,128)(2,1)} %vv_hbm.1, ...), custom_call_target="tpu_custom_call" | custom-call | tf_op jit(solution)/shard_map/pallas_call | solution.py:581
  96.5 0.0 copy-start
  96.5 2.7 %copy.12 = bf16[512,1536]{1,0:T(8,128)(2,1)} copy(bf16[512,1536]{1,0:T(8,128)(2,1)} %get-tuple-element.4) | data formatting | bytes 3145728
  99.2 0.0 copy-done
  99.2 0.7 copy.13
Async XLA Ops:
  96.5 2.7 %copy-start = (bf16[64,1536]{1,0:T(8,128)(2,1)S(1)}, bf16[64,1536]{1,0:T(8,128)(2,1)}, u32[]{:S(2)}) copy-start(bf16[64,1536]{1,0:T(8,128)(2,1)} %get-tuple-element.5) | copy-start | bytes 589828

commit v8 on v7

--- a/solution.py
+++ b/solution.py
@@ -22,19 +22,18 @@
 
 
 ORDER = (
-    "1Q0", "sQ1", "2Q0", "sK0", "1Q1", "3Q0", "2Q1", "sK1", "1K0", "3Q1", "4Q0", "sV0", "1K1", "1V0", "2K0",
-    "sV1", "4Q1", "ex", "A", -2, "2K1", -1, "1V1", "2V0", "3K0", "vqs", 2, "2V1", "3K1", "rQ1", 3, "3V0", 5,
-    "4K0", 6, "p0", 8, "4K1", "r1_0", "B", "p1", "r1_1", "X", -1, "rK1", 3, "3V1", "r2_0", "4V0", 6, "r2_1",
-    10, "ca_0", "4V1", "tw0", "T", "ca_1", "Y", 1, "cb_0", 2, "w0", "cb_1", "tw1", 3, "o_0", "w1", 4, "o_1",
-    5, "w2",
+    "1Q0", "sQ1", "fV", "2Q0", "1Q1", "sK0", "3Q0", "sK1", "2Q1", "1K0", "3Q1", "1K1", "4Q0", "sV0", "2K0",
+    "4Q1", "vqs", "2K1", "ex", "A", -2, "3K0", -1, "rQ1", 1, "3K1", 5, "4K0", 6, "3V0", "p0", "4K1", 7,
+    "sV1", "r1_0", "B", "p1", "r1_1", "X", 3, "3V1", 4, "rK1", 5, "r2_0", "r2_1", 10, "4V0", "ca_0", "ca_1",
+    "T", "4V1", "tw0", "Y", 1, "w0", "cb_0", 2, "cb_1", "tw1", 3, "w1", "o_0", 5, "w2", "o_1",
 )
 
 
 def kernel(
     clip_smem, video_clip, audio_clip, vq_hbm, vk_hbm, vv_hbm, aq_hbm, ak_hbm, av_hbm,
     vout_hbm, aout_hbm,
-    vq, vk, vv, ve, aq0, aq1, ak0, ak1, av0, av1, mk, am, mk_own, buf_c, buf_d, wt_c, wt_d, high_c, high_d, buf_a, buf_b, wb, tops, sums, window, part, got1, got2, vo, ao,
-    x_send, x_recv, g_send, g_recv, v_send, v_recv, v_local, r_send, r_recv, o_send, o_recv, w_send, w_recv, w_local,
+    vq, vk, vv, ve, aq0, aq1, ak0, ak1, av0, av1, v_row, mk, am, mk_own, buf_c, buf_d, wt_c, wt_d, high_c, high_d, buf_a, buf_b, wb, tops, sums, window, part, got1, got2, vo, ao,
+    x_send, x_recv, p_send, p_recv, p_local, g_send, g_recv, v_send, v_recv, v_local, r_send, r_recv, o_send, o_recv, w_send, w_recv, w_local,
 ):
     g = lax.axis_index("grp")
     s = lax.axis_index("seq")
@@ -87,18 +86,46 @@
     tensors = [(src, dst[half], half) for src, dst in ((aq_hbm, aq), (ak_hbm, ak), (av_hbm, av)) for half in (0, 1)]
     tensors.append((mk_own, mk, None))
 
+    def along(on_y, on_z):
+        return on_y * (1 - core) + on_z * core
+
+    u, up, um = along(y, z), along(yp, zp), along(ym, zm)
+    to_up = device(g, along(z, zp), along(yp, y), core)
+    to_um = device(g, along(z, zm), along(ym, y), core)
+    def ring(stage):
+        src, row = av_hbm, v_row
+        low, high = row.at[um, pl.ds(0, 32)], row.at[up, pl.ds(32, 32)]
+        plan = ((src, row.at[u], to_up), (src, row.at[u], to_um)) if stage == 0 else ((low, low, to_up), (high, high, to_um))
+        return [
+            remote(a, b, p_send.at[2 * stage + n], p_recv.at[2 * stage + n], dev) for n, (a, b, dev) in enumerate(plan)
+        ]
+
+    def ring_own():
+        return pltpu.make_async_copy(av_hbm, v_row.at[u], p_local)
+
     def x_copies(t, sender):
         src, dst, half = tensors[t]
-        return [
-            remote(
-                src if half is None else src.at[:, pl.ds(cc * 768 + half * 384, 384)], dst.at[sender, z, y], x_send.at[t, cc],
-                x_recv.at[t, sender], device(gm, z, y, cc),
-            )
-            for cc in (0, 1)
-        ]
-
-    def x_step(t):
-        return x_copies(t, core)
+        copies = []
+        for cc in (0, 1):
+            if half is None:
+                a, b = src, dst.at[sender, z, y]
+            elif t < 4:
+                a, b = src.at[:, pl.ds(cc * 768 + half * 384, 384)], dst.at[sender, z, y]
+            else:
+                a = v_row.at[:, :, pl.ds(cc * 768 + half * 384, 384)]
+                b = dst.at[0, z] if sender == 0 else dst.at[1, :, y]
+            copies.append(remote(a, b, x_send.at[t, cc], x_recv.at[t, sender], device(gm, z, y, cc)))
+        return copies
+
+    def x_start(t):
+        if t < 4 or t == 6:
+            start(x_copies(t, core))
+            return
+        for cc in (0, 1):
+
+            @pl.when(core == cc)
+            def _():
+                start(x_copies(t, cc))
 
     here_already = set()
 
@@ -176,14 +203,16 @@
     def swap_marks():
         return remote(ve.at[own_rows], ve.at[own_rows], v_send.at[3], v_recv.at[3], other)
 
-    start(x_step(0))
+    x_start(0)
+    start(ring(0))
+    ring_own().start()
     swap_start(0)
     swap_start(1)
 
     numbers = (audio_clip[...] - gm * CLIPS).astype(F32)
     numbers = jnp.concatenate([numbers, numbers], axis=1)
     mk_own[...] = jnp.broadcast_to(numbers, (32, HD)).astype(BF)
-    start(x_step(6))
+    x_start(6)
     clips = lax.broadcasted_iota(jnp.int32, (HD, HD), 0)
     for i in range(4):
         same = video_clip[i : i + 1, :] - g * CLIPS == clips
@@ -484,7 +513,7 @@
 
     def take(t, stage):
         for tensor in (6, 0) if t == 0 else (t,):
-            if stage == 0:
+            if stage == 0 or stage == 2 and 4 <= t < 6:
                 x_wait(tensor)
             else:
                 arrive(gather(tensor, stage - 1))
@@ -492,7 +521,14 @@
 
     def x_next(t):
         x_wait(t - 1)
-        start(x_step(t))
+        if t == 4:
+            arrive(ring(1))
+            ring_own().wait()
+        x_start(t)
+
+    def ring_next():
+        arrive(ring(0))
+        start(ring(1))
 
     def make_marks():
         arrive(gather(6, 3))
@@ -513,7 +549,7 @@
         start(results(half))
 
     steps = {
-        "vqs": lambda: swap_start(2), "ex": make_marks, "rQ1": lambda: arrive(gather(1, 3)), "rK1": lambda: arrive(gather(3, 3)),
+        "fV": ring_next, "vqs": lambda: swap_start(2), "ex": make_marks, "rQ1": lambda: arrive(gather(1, 3)), "rK1": lambda: arrive(gather(3, 3)),
         "tw0": lambda: arrive(gather(4, 3)), "tw1": lambda: arrive(gather(5, 3)),
         "w0": lambda: start(video_copies(0)), "w1": lambda: start(video_copies(1)), "w2": lambda: start(video_copies(2)),
     }
@@ -553,9 +589,11 @@
     video_values(parts["Y"])
 
     for t in range(7):
-        sent(x_step(t))
-        for stage in range(4):
+        sent(x_copies(t, 0))
+        for stage in (2, 3) if 4 <= t < 6 else range(4):
             sent(gather(t, stage))
+    sent(ring(0))
+    sent(ring(1))
     for i in range(3):
         swap(i)[0].wait_send()
     swap_marks().wait_send()
@@ -575,15 +613,18 @@
         away.wait()
 
 
+def hand_over(video_from, audio_from, video_to, audio_to):
+    video_to[...] = video_from[...]
+    audio_to[...] = audio_from[...]
+
+
 def on_device(video_q, video_k, video_v, audio_q, audio_k, audio_v, video_clip, audio_clip):
     anywhere = pl.BlockSpec(memory_space=pl.ANY)
     dma = pltpu.SemaphoreType.DMA
-    return pl.pallas_call(
+    results = (jax.ShapeDtypeStruct(video_q.shape, BF), jax.ShapeDtypeStruct(audio_k.shape, BF))
+    made = pl.pallas_call(
         kernel,
-        out_shape=(
-            jax.ShapeDtypeStruct(video_q.shape, BF),
-            jax.ShapeDtypeStruct(audio_k.shape, BF),
-        ),
+        out_shape=results,
         in_specs=[
             pl.BlockSpec(memory_space=pltpu.SMEM),
             pl.BlockSpec(memory_space=pltpu.VMEM),
@@ -602,6 +643,7 @@
             pltpu.VMEM((2, 4, 4, 64, 384), BF),
             pltpu.VMEM((2, 4, 4, 64, 384), BF),
             pltpu.VMEM((2, 4, 4, 64, 384), BF),
+            pltpu.VMEM((4, 64, 1536), BF),
             pltpu.VMEM((2, 4, 4, 32, HD), BF),
             pltpu.VMEM((2, 4, 4, 64, HD), BF),
             pltpu.VMEM((32, HD), BF),
@@ -624,6 +666,9 @@
             pltpu.VMEM((HD, 768), BF),
             dma((7, 2)),
             dma((7, 2)),
+            dma((4,)),
+            dma((4,)),
+            dma,
             dma((7, 16)),
             dma((7, 16)),
             dma((4,)),
@@ -644,6 +689,13 @@
         video_clip, video_clip.reshape(4, HD), audio_clip.reshape(1, 64), video_q, video_k, video_v, audio_q, audio_k,
         audio_v,
     )
+    return pl.pallas_call(
+        hand_over,
+        out_shape=results,
+        grid=(4,),
+        in_specs=[pl.BlockSpec((128, 1536), lambda i: (i, 0)), pl.BlockSpec((16, 1536), lambda i: (i, 0))],
+        out_specs=(pl.BlockSpec((128, 1536), lambda i: (i, 0)), pl.BlockSpec((16, 1536), lambda i: (i, 0))),
+    )(*made)
 
 
 def solution(mesh):

time: 100 us -> 98.5 us (0.985)
  local copies, waits for them, and re-layouts: 3.37 us -> 0 us
  Pallas kernels: 95.9 us -> 97.7 us
    unnamed x4 -> x0, local copies, waits for them, and re-layouts: 3.37 us -> none
    pallas_call x1 -> x2, Pallas kernels: 95.9 us -> 97.7 us  [the longest x1 94.1 us: on_device(): pl.pallas_call(kernel, out_shape=results, in_specs=[pl.BlockSpec(memory_s...]
where the time goes in v8:
time: 98.5 us; the launch traced here: 98.3 us
  Pallas kernels  97.7 us (99%)
    pallas_call x1, Pallas kernels, on_device(): pl.pallas_call(kernel, out_shape=results, in_specs=[pl.BlockSpec(memory_s...  94.1 us
    pallas_call x1, Pallas kernels, on_device(): pl.pallas_call(hand_over, out_shape=results, grid=(4,), in_specs=[pl.Bloc...  3.59 us

profile of v8, /device:TPU:1, one launch (start us, length us, event | category | flops | bytes accessed | tf_op | source)
XLA Modules:
  0.0 98.3 jit_solution(17733151931347814249)
XLA Ops:
  0.6 94.1 %shard_map.95 = (bf16[512,1536]{1,0:T(8,128)(2,1)}, bf16[64,1536]{1,0:T(8,128)(2,1)}) custom-call(s32[512]{0:T(512)} %clip_smem.1, s32[4,128]{1,0:T(4,128)} %bitcast.2, s32[1,64]{1,0:T(1,128)} %bitcast.3, bf16[512,1536]{1,0:T(8,128)(2,1)} %vq_hbm.1, bf16[512,1536]{1,0:T(8,128)(2,1)} %vk_hbm.1, bf16[512,1536]{1,0:T(8,128)(2,1)} %vv_hbm.1, ...), custom_call_target="tpu_custom_call" | custom-call | tf_op jit(solution)/shard_map/pallas_call | solution.py:625
  94.7 3.6 %shard_map.96 = (bf16[512,1536]{1,0:T(8,128)(2,1)}, bf16[64,1536]{1,0:T(8,128)(2,1)}) custom-call(bf16[512,1536]{1,0:T(8,128)(2,1)} %get-tuple-element.4.video_from, bf16[64,1536]{1,0:T(8,128)(2,1)} %get-tuple-element.5.audio_from), custom_call_target="tpu_custom_call" | custom-call | tf_op jit(solution)/shard_map/pallas_call | solution.py:692

commit v9 on v8

--- a/solution.py
+++ b/solution.py
@@ -613,9 +613,18 @@
         away.wait()
 
 
-def hand_over(video_from, audio_from, video_to, audio_to):
-    video_to[...] = video_from[...]
-    audio_to[...] = audio_from[...]
+def hand_over(video_from, audio_from, video_to, audio_to, video, audio, sem_in, sem_out):
+    pieces = [(video_from.at[r], video.at[r], video_to.at[r]) for r in (pl.ds(i * 128, 128) for i in range(4))]
+    pieces.append((audio_from, audio, audio_to))
+    arriving = [pltpu.make_async_copy(a, b, sem_in.at[i]) for i, (a, b, _) in enumerate(pieces)]
+    leaving = [pltpu.make_async_copy(b, c, sem_out.at[i]) for i, (_, b, c) in enumerate(pieces)]
+    for copy in arriving:
+        copy.start()
+    for into, out in zip(arriving, leaving):
+        into.wait()
+        out.start()
+    for copy in leaving:
+        copy.wait()
 
 
 def on_device(video_q, video_k, video_v, audio_q, audio_k, audio_v, video_clip, audio_clip):
@@ -692,9 +701,9 @@
     return pl.pallas_call(
         hand_over,
         out_shape=results,
-        grid=(4,),
-        in_specs=[pl.BlockSpec((128, 1536), lambda i: (i, 0)), pl.BlockSpec((16, 1536), lambda i: (i, 0))],
-        out_specs=(pl.BlockSpec((128, 1536), lambda i: (i, 0)), pl.BlockSpec((16, 1536), lambda i: (i, 0))),
+        in_specs=[anywhere] * 2,
+        out_specs=(anywhere, anywhere),
+        scratch_shapes=[pltpu.VMEM((512, 1536), BF), pltpu.VMEM((64, 1536), BF), dma((5,)), dma((5,))],
     )(*made)
 
 

time: 98.5 us -> 97.3 us (0.988)
  Pallas kernels: 97.7 us -> 96.4 us
    pallas_call x1, Pallas kernels: 3.59 us -> 2.28 us  [on_device(): pl.pallas_call(hand_over, out_shape=results, in_specs=[anywhere] * 2, out...]
where the time goes in v9:
time: 97.3 us; the launch traced here: 97.2 us
  Pallas kernels  96.4 us (99%)
    pallas_call x1, Pallas kernels, on_device(): pl.pallas_call(kernel, out_shape=results, in_specs=[pl.BlockSpec(memory_s...  94.1 us
    pallas_call x1, Pallas kernels, on_device(): pl.pallas_call(hand_over, out_shape=results, in_specs=[anywhere] * 2, out...  2.28 us

profile of v9, /device:TPU:1, one launch (start us, length us, event | category | flops | bytes accessed | tf_op | source)
XLA Modules:
  0.0 97.2 jit_solution(3468261875253830081)
XLA Ops:
  0.6 94.1 %shard_map.95 = (bf16[512,1536]{1,0:T(8,128)(2,1)}, bf16[64,1536]{1,0:T(8,128)(2,1)}) custom-call(s32[512]{0:T(512)} %clip_smem.1, s32[4,128]{1,0:T(4,128)} %bitcast.2, s32[1,64]{1,0:T(1,128)} %bitcast.3, bf16[512,1536]{1,0:T(8,128)(2,1)} %vq_hbm.1, bf16[512,1536]{1,0:T(8,128)(2,1)} %vk_hbm.1, bf16[512,1536]{1,0:T(8,128)(2,1)} %vv_hbm.1, ...), custom_call_target="tpu_custom_call" | custom-call | tf_op jit(solution)/shard_map/pallas_call | solution.py:634
  94.7 2.3 %shard_map.96 = (bf16[512,1536]{1,0:T(8,128)(2,1)}, bf16[64,1536]{1,0:T(8,128)(2,1)}) custom-call(bf16[512,1536]{1,0:T(8,128)(2,1)} %get-tuple-element.4.video_from, bf16[64,1536]{1,0:T(8,128)(2,1)} %get-tuple-element.5.audio_from), custom_call_target="tpu_custom_call" | custom-call | tf_op jit(solution)/shard_map/pallas_call | solution.py:701

commit v10 on v9

--- a/solution.py
+++ b/solution.py
@@ -459,14 +459,16 @@
         return cols, pl.ds(pl.multiple_of(lax.rem(u, 2) * 512, 512), 512)
 
     def video_both(u_scores, ref, u_out, buf_scores, buf_out):
-        cols, here = video_unit(u_scores)
-        q = jnp.concatenate([vq[here, cols], ve[here, :]], axis=1)
+        if u_scores is not None:
+            cols, here = video_unit(u_scores)
+            q = jnp.concatenate([vq[here, cols], ve[here, :]], axis=1)
         row = 0
         for c in range(5):
-            k = jnp.concatenate([rows_of(ref, c, u_scores // 2), rows_of(am, c, None)], axis=1)
-            buf_scores[:, c * 256 : (c + 1) * 256] = lax.dot_general(
-                q, k, (((1,), (1,)), ((), ())), preferred_element_type=F32
-            )
+            if u_scores is not None:
+                k = jnp.concatenate([rows_of(ref, c, u_scores // 2), rows_of(am, c, None)], axis=1)
+                buf_scores[:, c * 256 : (c + 1) * 256] = lax.dot_general(
+                    q, k, (((1,), (1,)), ((), ())), preferred_element_type=F32
+                )
             if u_out is not None:
                 for _ in range(7 if c < 2 else 6):
                     scores = buf_out[row : row + 16, :]
@@ -479,7 +481,7 @@
             u = 2 * i
             video_both(u + 1, refs[0], u, buf_b, buf_a)
             run_events(u, events, range(lo, hi, 2))
-            video_both(jnp.minimum(u + 2, 11), refs[1], u + 1, buf_a, buf_b)
+            video_both(u + 2, refs[1], u + 1, buf_a, buf_b)
             run_events(u + 1, events, range(lo + 1, hi, 2))
             return carry
 
@@ -487,7 +489,11 @@
         run_now(-1, events)
         lax.fori_loop(0, 2, functools.partial(body, (ak[0], ak[0]), 0, 4), 0)
         lax.fori_loop(2, 3, functools.partial(body, (ak[0], ak[1]), 4, 6), 0)
-        lax.fori_loop(3, 6, functools.partial(body, (ak[1], ak[1]), 6, 12), 0)
+        lax.fori_loop(3, 5, functools.partial(body, (ak[1], ak[1]), 6, 10), 0)
+        video_both(11, ak[1], 10, buf_b, buf_a)
+        run_now(10, events)
+        video_both(None, None, 11, None, buf_b)
+        run_now(11, events)
 
     def video_values(events):
         def body(ref, lo, hi, i, carry):

time: 97.3 us -> 97.3 us (level)
  no operation moved by 1% of the time
where the time goes in v10:
time: 97.3 us; the launch traced here: 97.2 us
  Pallas kernels  96.4 us (99%)
    pallas_call x1, Pallas kernels, on_device(): pl.pallas_call(kernel, out_shape=results, in_specs=[pl.BlockSpec(memory_s...  94.1 us
    pallas_call x1, Pallas kernels, on_device(): pl.pallas_call(hand_over, out_shape=results, in_specs=[anywhere] * 2, out...  2.28 us

profile of v10, /device:TPU:1, one launch (start us, length us, event | category | flops | bytes accessed | tf_op | source)
XLA Modules:
  0.0 97.2 jit_solution(8143665861806367911)
XLA Ops:
  0.6 94.1 %shard_map.95 = (bf16[512,1536]{1,0:T(8,128)(2,1)}, bf16[64,1536]{1,0:T(8,128)(2,1)}) custom-call(s32[512]{0:T(512)} %clip_smem.1, s32[4,128]{1,0:T(4,128)} %bitcast.2, s32[1,64]{1,0:T(1,128)} %bitcast.3, bf16[512,1536]{1,0:T(8,128)(2,1)} %vq_hbm.1, bf16[512,1536]{1,0:T(8,128)(2,1)} %vk_hbm.1, bf16[512,1536]{1,0:T(8,128)(2,1)} %vv_hbm.1, ...), custom_call_target="tpu_custom_call" | custom-call | tf_op jit(solution)/shard_map/pallas_call | solution.py:640
  94.7 2.3 %shard_map.96 = (bf16[512,1536]{1,0:T(8,128)(2,1)}, bf16[64,1536]{1,0:T(8,128)(2,1)}) custom-call(bf16[512,1536]{1,0:T(8,128)(2,1)} %get-tuple-element.4.video_from, bf16[64,1536]{1,0:T(8,128)(2,1)} %get-tuple-element.5.audio_from), custom_call_target="tpu_custom_call" | custom-call | tf_op jit(solution)/shard_map/pallas_call | solution.py:707
